TPU v7x, 32 devices: a whole 2x2x4 slice. The times are simulated.
32 devices in a mesh: group: 2 (over x), rx: 16 (over z, y, core).
Axes of the slice: x: 2, y: 2, z: 4, core: 2. Of those that a mesh axis runs over, the one named last changes fastest.
Arguments:
- traces: bfloat16 [1024, 2, 512], P('rx', 'group'), parts along dimension 1, may hold values from -6 to 6
- cotangent: bfloat16 [1024, 2, 512], P('rx', 'group'), parts along dimension 1, may hold values from -6 to 6
- mute_mask: int32 [1024, 2], P('rx', 'group'), parts along dimension 1, may hold values 0 or 1
- dead_flags: int32 [1024], P('rx'), may hold values 0 or 1
- first_conv_weights: float32 [3, 64], replicated, may hold values from -3.5 to 3.5
- first_bias: float32 [64], replicated, may hold values from -3 to 3
- conv_taps: bfloat16 [3, 64, 64], replicated, may hold values from -0.4375 to 0.4375
- in_proj: bfloat16 [64, 64], replicated, may hold values from -0.1875 to 0.1875
- out_proj: bfloat16 [64, 64], replicated, may hold values from -0.1875 to 0.1875
- decay_rates: float32 [64], replicated, may hold values from 0 to 0.12
- low_rank: float32 [64], replicated, may hold values from -4 to 4
- mix_weights: float32 [64], replicated, may hold values from -0.75 to 0.75
- back_weights: float32 [64], replicated, may hold values from -4 to 4
- read_weights: float32 [64], replicated, may hold values from -0.75 to 0.75
- down_basis: bfloat16 [256, 1024], P(None, 'rx'), may hold values from -0.125 to 0.125
- up_basis: bfloat16 [1024, 256], P('rx'), may hold values from -0.5 to 0.5
Outputs:
- predicted: float32 [1024, 2, 512], P('rx', 'group'), parts along dimension 1
- grad_conv: float32 [6, 64, 64], P('group'), parts along dimension 0
- grad_in: float32 [128, 64], P('group'), parts along dimension 0
- grad_out: float32 [128, 64], P('group'), parts along dimension 0
- grad_down: float32 [512, 1024], P('group', 'rx'), parts along dimension 0
- grad_up: float32 [1024, 512], P('rx', 'group'), parts along dimension 1
There are 2 independent parts, one for each index of `group`. A program takes and returns all parts, laid end to end along the dimension named above; an argument that names none is the same for every part. Nothing has to cross between parts.
All inputs are finite; a program needn't handle non-finite values. No bound on the sum of `mute_mask` or of `dead_flags` on one device may be relied on, other than what follows from the above.
Results may differ from a plain program's by a relative error of at most 0.02.
Values may be sent and summed in bfloat16 or wider, within the bound.
A program may use at most 128 MiB of HBM per device.

v0:
```python
import jax
import jax.numpy as jnp
from jax import lax
from jax.sharding import PartitionSpec as P

FIRST_DILATION = 1
SECOND_DILATION = 4


BETA = 0.5
HIGH = lax.Precision.HIGHEST


def carried_in(x, axis, combine, identity, reverse):
    devices, mine = (lax.axis_size(axis), lax.axis_index(axis))
    everything = jax.tree.map(lambda part: lax.all_gather(part, axis), x)
    start = jax.tree.map(
        lambda part, zero: jnp.broadcast_to(jnp.asarray(zero, part.dtype), part.shape), x, identity
    )

    def hop(k, before):
        at = devices - 1 - k if reverse else k
        reached = at > mine if reverse else at < mine
        new = combine(before, jax.tree.map(lambda part: part[at], everything))
        return jax.tree.map(lambda a, b: jnp.where(reached, a, b), new, before)

    return lax.fori_loop(0, devices, hop, start)


def time_delay_samples(values, offset):
    if offset == 0:
        return values
    length = values.shape[-1]
    filler = jnp.zeros(values.shape[:-1] + (abs(offset),), values.dtype)
    if offset > 0:
        return jnp.concatenate([values[..., offset:], filler], axis=-1)
    return jnp.concatenate([filler, values[..., : length + offset]], axis=-1)


def silu_slope(values):
    logistic = jax.nn.sigmoid(values)
    return logistic * (1.0 + values * (1.0 - logistic))


def apply_decay(current, gain_row, decay_rows, unit_vector):
    projected = jnp.einsum("n,snt->st", unit_vector, current, precision=HIGH)
    return gain_row[:, None, None] * (
        decay_rows[None, :, None] * current
        - BETA * unit_vector[None, :, None] * projected[:, None, :]
    )


def chain_combine(earlier, later):
    matrix = jnp.einsum("snm,smk->snk", later[0], earlier[0], precision=HIGH)
    vector = jnp.einsum("snm,smt->snt", later[0], earlier[1], precision=HIGH) + later[1]
    return (matrix, vector)


def per_device(
    traces,
    cotangent,
    mute_mask,
    dead_flags,
    first_conv_weights,
    first_bias,
    conv_taps,
    in_proj,
    out_proj,
    decay_rates,
    low_rank,
    mix_weights,
    back_weights,
    read_weights,
    down_basis,
    up_basis,
):
    shots = traces.shape[1]
    window = traces.shape[2]
    width = first_conv_weights.shape[1]
    states_n = in_proj.shape[0]
    filter_weights = first_conv_weights.shape[0]
    input_trace = traces.astype(jnp.float32) * (1.0 - dead_flags.astype(jnp.float32))[:, None, None]
    first_conv_output = (
        jnp.zeros(input_trace.shape[:2] + (width, window), jnp.float32)
        + first_bias[None, None, :, None]
    )
    for filter_tap in range(filter_weights):
        first_conv_output = (
            first_conv_output
            + first_conv_weights[filter_tap][None, None, :, None]
            * time_delay_samples(input_trace, (filter_tap - 1) * FIRST_DILATION)[:, :, None, :]
        )
    first_hidden_layer = jax.nn.silu(first_conv_output).astype(jnp.bfloat16)
    delayed_trace_list = [
        time_delay_samples(first_hidden_layer, (filter_tap - 1) * SECOND_DILATION)
        for filter_tap in range(filter_weights)
    ]
    pre_two = jnp.zeros(first_hidden_layer.shape, jnp.float32)
    for filter_tap in range(filter_weights):
        pre_two = pre_two + jnp.einsum(
            "dc,rsct->rsdt",
            conv_taps[filter_tap],
            delayed_trace_list[filter_tap],
            preferred_element_type=jnp.float32,
        )
    hidden_two = (first_hidden_layer.astype(jnp.float32) + jax.nn.silu(pre_two)).astype(
        jnp.bfloat16
    )
    raw_drive = jnp.einsum("nc,rsct->rsnt", in_proj, hidden_two, preferred_element_type=jnp.float32)
    drive = raw_drive - jnp.mean(raw_drive, axis=-1, keepdims=True)
    decay_rows = jnp.exp(-decay_rates)
    unit_vector = low_rank * lax.rsqrt(jnp.sum(low_rank * low_rank) + 1e-06)
    gains = 1.0 - 0.25 * mute_mask.astype(jnp.float32)
    base_matrix = jnp.diag(decay_rows) - BETA * jnp.outer(unit_vector, unit_vector)
    identity_mats = jnp.broadcast_to(
        jnp.eye(states_n, dtype=jnp.float32), (shots, states_n, states_n)
    )
    zeros_state = jnp.zeros((shots, states_n, window), jnp.float32)

    def matrix_step(product, gain_row):
        product = jnp.einsum(
            "snm,smk->snk", gain_row[:, None, None] * base_matrix[None], product, precision=HIGH
        )
        return (product, product)

    through, partials = lax.scan(matrix_step, identity_mats, gains)

    def forward_step(current, inputs):
        drive_row, gain_row = inputs
        current = apply_decay(current, gain_row, decay_rows, unit_vector) + drive_row
        return (current, current)

    local_end, local_states = lax.scan(forward_step, zeros_state, (drive, gains))
    entering = carried_in(
        (through, local_end), "rx", chain_combine, (identity_mats, zeros_state), False
    )
    final_state, states = lax.scan(forward_step, entering[1], (drive, gains))
    states_low = states.astype(jnp.bfloat16)
    mixed = hidden_two.astype(jnp.float32) + jnp.einsum(
        "cn,rsnt->rsct", out_proj, states_low, preferred_element_type=jnp.float32
    )
    summary = jnp.einsum("c,rsct->rst", mix_weights, mixed, precision=HIGH).astype(jnp.bfloat16)
    whole_terms = jnp.einsum("kr,rst->kst", down_basis, summary, preferred_element_type=jnp.float32)
    bottleneck = lax.psum(whole_terms, "rx")
    active = jnp.tanh(bottleneck).astype(jnp.bfloat16)
    spread = jnp.einsum("rk,kst->rst", up_basis, active, preferred_element_type=jnp.float32)
    coupling = jnp.sum(read_weights * back_weights)
    predicted = jnp.einsum("c,rsct->rst", read_weights, mixed, precision=HIGH) + coupling * spread
    spread_grad = (coupling * cotangent.astype(jnp.float32)).astype(jnp.bfloat16)
    whole_grads = jnp.einsum(
        "rk,rst->kst", up_basis, spread_grad, preferred_element_type=jnp.float32
    )
    active_grad = lax.psum(whole_grads, "rx")
    bottle_grad = (active_grad * (1.0 - jnp.square(active.astype(jnp.float32)))).astype(
        jnp.bfloat16
    )
    grad_up = jnp.einsum("rst,kst->rk", spread_grad, active, preferred_element_type=jnp.float32)
    grad_down = jnp.einsum("kst,rst->kr", bottle_grad, summary, preferred_element_type=jnp.float32)
    summary_grad = jnp.einsum(
        "kr,kst->rst", down_basis, bottle_grad, preferred_element_type=jnp.float32
    )
    mixed_grad = (
        read_weights[None, None, :, None] * cotangent.astype(jnp.float32)[:, :, None, :]
        + mix_weights[None, None, :, None] * summary_grad[:, :, None, :]
    )
    mixed_low = mixed_grad.astype(jnp.bfloat16)
    source = jnp.einsum("cn,rsct->rsnt", out_proj, mixed_low, preferred_element_type=jnp.float32)

    def backward_step(incoming, inputs):
        source_row, gain_row = inputs
        adjoint = source_row + incoming
        return (apply_decay(adjoint, gain_row, decay_rows, unit_vector), adjoint)

    leaving, local_adjoints = lax.scan(backward_step, zeros_state, (source, gains), reverse=True)
    arriving = carried_in(
        (jnp.swapaxes(through, 1, 2), leaving),
        "rx",
        chain_combine,
        (identity_mats, zeros_state),
        True,
    )
    first_carry, adjoints = lax.scan(backward_step, arriving[1], (source, gains), reverse=True)
    adjoints_low = adjoints.astype(jnp.bfloat16)
    adjoint_totals = jnp.sum(adjoints_low.astype(jnp.float32), axis=-1)
    hidden_means = jnp.mean(hidden_two.astype(jnp.float32), axis=-1)
    local_out = jnp.einsum(
        "rsct,rsnt->cn", mixed_low, states_low, preferred_element_type=jnp.float32
    )
    local_in = jnp.einsum(
        "rsnt,rsct->nc", adjoints_low, hidden_two, preferred_element_type=jnp.float32
    ) - jnp.einsum("rsn,rsc->nc", adjoint_totals, hidden_means, precision=HIGH)
    back_proj = jnp.einsum(
        "nc,rsnt->rsct", in_proj, adjoints_low, preferred_element_type=jnp.float32
    )
    hidden_grad = mixed_grad + back_proj - jnp.mean(back_proj, axis=-1, keepdims=True)
    pre_grad = (hidden_grad * silu_slope(pre_two)).astype(jnp.bfloat16)
    tap_grads = []
    for filter_tap in range(filter_weights):
        tap_grads.append(
            jnp.einsum(
                "rsdt,rsct->dc",
                pre_grad,
                delayed_trace_list[filter_tap],
                preferred_element_type=jnp.float32,
            )
        )
    local_conv = jnp.stack(tap_grads, axis=0)
    grad_conv, grad_in, grad_out = lax.psum((local_conv, local_in, local_out), "rx")
    return (predicted, grad_conv, grad_in, grad_out, grad_down, grad_up)


def solution(mesh):
    return jax.shard_map(
        per_device,
        mesh=mesh,
        in_specs=(
            P("rx", "group", None),
            P("rx", "group", None),
            P("rx", "group"),
            P("rx"),
            P(),
            P(),
            P(),
            P(),
            P(),
            P(),
            P(),
            P(),
            P(),
            P(),
            P(None, "rx"),
            P("rx", None),
        ),
        out_specs=(
            P("rx", "group", None),
            P("group", None, None),
            P("group", None),
            P("group", None),
            P("group", "rx"),
            P("rx", "group"),
        ),
        check_vma=False,
    )
```

profile of v0, /device:TPU:0, one launch (start us, length us, event | category | flops | bytes accessed | tf_op | source)
XLA Modules:
  0.0 1254.0 jit_solution(6670205354568349589)
XLA Ops:
  9.8 4.1 multiply_convert_fusion.1
  13.9 3.9 fusion.169
  17.9 6.5 fusion.107
  24.4 4.5 fusion.87
  30.2 13.2 %convert_reduce_fusion = (f32[64,64]{1,0:T(8,128)S(1)}, bf16[64,1,64,512]{3,2,0,1:T(8,128)(2,1)S(1)}, f32[64,512,64]{1,2,0:T(8,128)}) fusion(f32[64,512]{1,0:T(8,128)S(1)} %get-tuple-element.866, f32[64]{0:T(128)S(1)} %get-tuple-element.859, f32[64,512]{1,0:T(8,128)S(1)} %get-tuple-element.856, f32[64]{0:T(128)S(1)} %get-tuple-element.860, ...), kind=kOutput, calls=%fused_computation.73 | convolution fusion | flops 314568704 | bytes 33949696 | tf_op jit(solution)/shard_map/dc,rsct->rsdt/dot_general | solution.py:100
  44.8 3.6 fusion.56
  48.5 156.0 %while.98 = (s32[]{:T(128)}, f32[1,64,512]{2,1,0:T(8,128)S(1)}, f32[64,1]{0,1:T(1,128)S(1)}, f32[64]{0:T(128)S(1)}, f32[64]{0:T(128)S(1)}, /*index=5*/f32[64,1,64,512]{3,2,1,0:T(8,128)}, s32[]{:T(128)}, s32[]{:T(128)}) while((s32[]{:T(128)}, f32[1,64,512]{2,1,0:T(8,128)S(1)}, f32[64,1]{0,1:T(1,128)S(1)}, f32[64]{0:T(128)S(1)}, ...), condition=%wide.region_5.6_spmd.clone, body=%wide.region_4.5_spmd.clone.sunk | while | flops 622659 | bytes 529788 | solution.py:133
  207.8 95.2 %while.97 = (s32[]{:T(128)}, f32[1,64,64]{2,1,0:T(8,128)S(1)}, f32[64,1]{0,1:T(1,128)S(1)}, f32[64]{0:T(128)S(1)}, f32[64]{0:T(128)S(1)}, /*index=5*/s32[]{:T(128)}) while((s32[]{:T(128)}, f32[1,64,64]{2,1,0:T(8,128)S(1)}, f32[64,1]{0,1:T(1,128)S(1)}, f32[64]{0:T(128)S(1)}, f32[64]{0:T(128)S(1)}, /*index=5*/s32[]{:T(128)}) %tuple.254), condition=%wide.region_2.3_spmd.clone, body=%wide.region_1.2_spmd.clone.sunk | while | flops 3170306 | bytes 66141 | solution.py:126
  303.0 24.6 %all-gather = f32[16,64,64]{2,1,0:T(8,128)S(1)} all-gather(f32[1,64,64]{2,1,0:T(8,128)S(1)} %get-tuple-element.586), channel_id=2, replica_groups=mesh['group'=2,'rx'=16] {'rx'}, dimensions={0}, use_global_device_ids=true | all-gather | bytes 278528 | tf_op jit(solution)/shard_map/all_gather | solution.py:16
  327.6 19.7 %while.99 = (s32[]{:T(128)}, f32[1,64,512]{2,1,0:T(8,128)S(1)}, s32[]{:T(128)}, f32[16,1,64,64]{3,2,1,0:T(8,128)S(1)}, f32[16,1,64,512]{3,2,1,0:T(8,128)}, /*index=5*/s32[]{:T(128)}, s32[]{:T(128)}) while((s32[]{:T(128)}, f32[1,64,512]{2,1,0:T(8,128)S(1)}, s32[]{:T(128)}, f32[16,1,64,64]{3,2,1,0:T(8,128)S(1)}, ...), condition=%wide.region_7.8_spmd.clone, body=%wide.region_6.7_spmd.clone.sunk | while | flops 25296900 | bytes 821863 | solution.py:27
  347.3 2.5 broadcast.488.clone
  349.8 195.6 %while.95 = (s32[]{:T(128)}, f32[1,64,512]{2,1,0:T(8,128)S(1)}, bf16[64,1,64,512]{3,2,1,0:T(8,128)(2,1)}, f32[64,1]{0,1:T(1,128)S(1)}, f32[64]{0:T(128)S(1)}, /*...) while((s32[]{:T(128)}, f32[1,64,512]{2,1,0:T(8,128)S(1)}, bf16[64,1,64,512]{3,2,1,0:T(8,128)(2,1)}, ...), condition=%wide.region_9.10_spmd, body=%wide.region_8.9_spmd.sunk | while | flops 557122 | bytes 661357 | solution.py:137
  359.7 2.3 bitcast_dynamic-update-slice_fusion.4
  365.8 2.3 bitcast_dynamic-update-slice_fusion.4
  368.9 2.3 bitcast_dynamic-update-slice_fusion.4
  381.1 2.3 bitcast_dynamic-update-slice_fusion.4
  387.2 2.3 bitcast_dynamic-update-slice_fusion.4
  390.3 2.3 bitcast_dynamic-update-slice_fusion.4
  402.5 2.3 bitcast_dynamic-update-slice_fusion.4
  414.7 2.3 bitcast_dynamic-update-slice_fusion.4
  430.0 2.3 bitcast_dynamic-update-slice_fusion.4
  433.0 2.3 bitcast_dynamic-update-slice_fusion.4
  436.1 2.3 bitcast_dynamic-update-slice_fusion.4
  454.4 2.3 bitcast_dynamic-update-slice_fusion.4
  463.6 2.3 bitcast_dynamic-update-slice_fusion.4
  472.8 2.3 bitcast_dynamic-update-slice_fusion.4
  478.9 2.3 bitcast_dynamic-update-slice_fusion.4
  503.3 2.3 bitcast_dynamic-update-slice_fusion.4
  518.6 2.3 bitcast_dynamic-update-slice_fusion.4
  524.7 2.3 bitcast_dynamic-update-slice_fusion.4
  527.8 2.3 bitcast_dynamic-update-slice_fusion.4
  543.1 2.3 bitcast_dynamic-update-slice_fusion.4
  545.4 3.6 fusion.81
  549.0 3.2 copy-done.1
  552.2 4.9 fusion.64
  558.3 90.6 %all-reduce.11.cloned.1.call-done = (f32[256,1,512]{0,2,1:T(8,128)}, f32[256,1,512]{0,2,1:T(8,128)}) async-done(((f32[256,1,512]{0,2,1:T(8,128)}, f32[256,1,512]{0,2,1:T(8,128)}), (f32[256,1,512]{0,2,1:T(8,128)}, f32[256,1,512]{0,2,1:T(8,128)})) %all-reduce.11.cloned.1.call-update) | async-done | bytes 1048592 | tf_op jit(solution)/shard_map/psum | solution.py:144
  650.4 4.7 fusion.104
  655.2 215.5 %while.100 = (s32[]{:T(128)}, f32[1,64,512]{2,1,0:T(8,128)S(1)}, f32[64,1]{0,1:T(1,128)S(1)}, f32[64]{0:T(128)S(1)}, f32[64,1,64,512]{3,2,1,0:T(8,128)}, /*index...) while((s32[]{:T(128)}, f32[1,64,512]{2,1,0:T(8,128)S(1)}, f32[64,1]{0,1:T(1,128)S(1)}, ...), condition=%wide.region_14.15_spmd.clone, body=%wide.region_13.14_spmd.clone.sunk | while | flops 655428 | bytes 660884 | solution.py:174
  871.5 21.9 %all-gather.2 = f32[16,64,64]{2,1,0:T(8,128)S(1)} all-gather(f32[1,64,64]{2,1,0:T(8,128)S(1)} %bitcast.392), channel_id=4, replica_groups=mesh['group'=2,'rx'=16] {'rx'}, dimensions={0}, use_global_device_ids=true | all-gather | bytes 278528 | tf_op jit(solution)/shard_map/all_gather | solution.py:16
  893.4 7.8 fusion.66
  905.5 7.3 all-gather.9.cloned.1.call-done
  912.8 19.7 %while.101 = (s32[]{:T(128)}, f32[1,64,512]{2,1,0:T(8,128)S(1)}, s32[]{:T(128)}, f32[16,1,64,64]{3,2,1,0:T(8,128)S(1)}, f32[16,1,64,512]{3,2,1,0:T(8,128)}, /*index=5*/s32[]{:T(128)}, s32[]{:T(128)}, s32[]{:T(128)}, s32[]{:T(128)}) while((s32[]{:T(128)}, f32[1,64,512]{2,1,0:T(8,128)S(1)}, s32[]{:T(128)}, ...), condition=%wide.region_16.17_spmd.clone, body=%wide.region_15.16_spmd.clone.sunk | while | flops 25296904 | bytes 821925 | solution.py:27
  932.5 2.5 broadcast.488
  935.0 196.9 %while.96 = (s32[]{:T(128)}, f32[1,64,512]{2,1,0:T(8,128)S(1)}, bf16[64,1,64,512]{3,2,1,0:T(8,128)(2,1)}, f32[64,1]{0,1:T(1,128)S(1)}, f32[64]{0:T(128)S(1)}, /*...) while((s32[]{:T(128)}, f32[1,64,512]{2,1,0:T(8,128)S(1)}, ...), condition=%wide.region_18.19_spmd, body=%wide.region_17.18_spmd.sunk | while | flops 557123 | bytes 923013 | solution.py:182
  1131.9 4.3 bitcast_reduce_fusion
  1136.3 7.1 fusion.55
  1144.6 4.1 fusion.123
  1157.2 85.6 %all-reduce.9.cloned.1.call-done = (f32[3,64,64]{2,1,0:T(8,128)}, f32[64,64]{1,0:T(8,128)}, f32[64,64]{1,0:T(8,128)}) async-done(((f32[3,64,64]{2,1,0:T(8,128)}, f32[64,64]{1,0:T(8,128)}, f32[64,64]{1,0:T(8,128)}), (f32[3,64,64]{2,1,0:T(8,128)}, f32[64,64]{1,0:T(8,128)}, f32[64,64]{1,0:T(8,128)})) %all-reduce.9.cloned.1.call-update) | async-done | bytes 81936 | tf_op jit(solution)/shard_map/psum | solution.py:208
  (1419 shorter events, 872.9 us)
Async XLA Ops:
  7.2 549.9 %copy-start = (bf16[256,64]{0,1:T(8,128)(2,1)S(1)}, bf16[256,64]{0,1:T(8,128)(2,1)}, u32[]{:S(2)}) copy-start(bf16[256,64]{0,1:T(8,128)(2,1)} %param.44) | copy-start | bytes 98308
  7.2 320.4 %all-gather.7.cloned.1.call-start = ((), (), s32[]{:S(2)}) async-start(), calls=%async_computation | async-start | bytes 2228224 | tf_op jit(solution)/shard_map/all_gather | solution.py:16
  13.9 4.0 copy-start.17
  13.9 4.0 copy-start.20
  17.9 6.5 copy-start.6
  24.4 4.5 copy-start.23
  24.4 4.5 copy-start.22
  30.2 13.2 %copy-start.16 = (bf16[64,64]{1,0:T(8,128)(2,1)S(1)}, bf16[64,64]{1,0:T(8,128)(2,1)}, u32[]{:S(2)}) copy-start(bf16[64,64]{1,0:T(8,128)(2,1)} %param.37) | copy-start | bytes 24580
  43.4 5.1 copy-start.2
  43.4 1.3 copy-start.21
  44.8 160.6 %copy-start.18 = (f32[64]{0:T(128)S(1)}, f32[64]{0:T(128)}, u32[]{:S(2)}) copy-start(f32[64]{0:T(128)} %param.43) | copy-start | bytes 772
  44.8 160.6 %copy-start.24 = (f32[64]{0:T(128)S(1)}, f32[64]{0:T(128)}, u32[]{:S(2)}) copy-start(f32[64]{0:T(128)} %param.42) | copy-start | bytes 772
  44.8 161.3 %copy-start.13 = (bf16[64,1,512]{2,0,1:T(8,128)(2,1)S(1)}, bf16[64,1,512]{2,0,1:T(8,128)(2,1)}, u32[]{:S(2)}) copy-start(bf16[64,1,512]{2,0,1:T(8,128)(2,1)} %param.31) | copy-start | bytes 196612
  44.8 161.3 %copy-start.14 = (bf16[64,256]{1,0:T(8,128)(2,1)S(1)}, bf16[64,256]{1,0:T(8,128)(2,1)}, u32[]{:S(2)}) copy-start(bf16[64,256]{1,0:T(8,128)(2,1)} %param.45) | copy-start | bytes 98308
  48.5 496.9 %copy-start.15 = (bf16[64,64]{1,0:T(8,128)(2,1)S(1)}, bf16[64,64]{1,0:T(8,128)(2,1)}, u32[]{:S(2)}) copy-start(bf16[64,64]{1,0:T(8,128)(2,1)} %param.38) | copy-start | bytes 24580
  204.4 0.7 copy-start.10
  205.1 443.8 %all-reduce.11.cloned.1.call-start = ((), (), s32[]{:S(2)}) async-start(), calls=%async_computation.3 | async-start | bytes 2097152 | tf_op jit(solution)/shard_map/psum | solution.py:144
  349.8 202.4 %copy-start.19 = (f32[64]{0:T(128)S(1)}, f32[64]{0:T(128)}, u32[]{:S(2)}) copy-start(f32[64]{0:T(128)} %param.41) | copy-start | bytes 772
  545.4 6.8 copy-start.3
  548.9 3.2 copy-start.1
  558.2 354.6 %all-gather.9.cloned.1.call-start = ((), (), s32[]{:S(2)}) async-start(), calls=%async_computation.1 | async-start | bytes 2228224 | tf_op jit(solution)/shard_map/all_gather | solution.py:16
  655.2 246.9 %copy-start.12 = (f32[256,1,512]{0,2,1:T(8,128)S(1)}, f32[256,1,512]{0,2,1:T(8,128)}, u32[]{:S(2)}) copy-start(f32[256,1,512]{0,2,1:T(8,128)} %get-tuple-element.844) | copy-start | bytes 1572868
  870.7 0.7 copy-start.11
  871.3 371.5 %all-reduce.9.cloned.1.call-start = ((), (), s32[]{:S(2)}) async-start(), calls=%async_computation.2 | async-start | bytes 327680 | tf_op jit(solution)/shard_map/psum | solution.py:208
  871.5 32.1 %copy-start.8 = (bf16[64,1,64,512]{3,2,1,0:T(8,128)(2,1)S(1)}, bf16[64,1,64,512]{3,2,1,0:T(8,128)(2,1)}, u32[]{:S(2)}) copy-start(bf16[64,1,64,512]{3,2,1,0:T(8,128)(2,1)} %get-tuple-element.589) | copy-start | bytes 12582916
  1136.2 7.1 copy-start.7
  1144.6 4.1 copy-start.9
  1148.6 2.2 copy-start.4
  1148.6 3.5 copy-start.5
Sparse Core Ops, SparseCore 0:
  205.2 44.1 all-gather.6
  558.3 90.5 all-reduce.10
  871.5 41.2 all-gather.8
  1155.6 87.1 all-reduce.8
where the time goes:
time: 1270 us; the launch traced here: 1250 us
  other arithmetic  523 us (41%)
  matrix products  265 us (21%)
  local copies, waits for them, and re-layouts  211 us (17%)
  waiting for transfers between devices  184 us (14%)
  blocking collectives  46.5 us (4%)
  between operations  15.3 us (1%)
    dynamic_update_slice x128, other arithmetic, per_device(): final_state, states = lax.scan(forward_step, entering[1], (drive, gains))  245 us
    dynamic_slice x320, local copies, waits for them, and re-layouts, per_device(): through, partials = lax.scan(matrix_step, identity_mats, gains)  189 us
    mul x128, other arithmetic, apply_decay(): gain_row[:, None, None]  152 us
    dot_general x256, matrix products, apply_decay(): projected = jnp.einsum('n,snt->st', unit_vector, current, precision=HIGH)  105 us
    add x64, other arithmetic, forward_step(): apply_decay(current, gain_row, decay_rows, unit_vector) + drive_row  105 us
    psum x1, waiting for transfers between devices, per_device(): bottleneck = lax.psum(whole_terms, 'rx')  90.6 us
    psum x1, waiting for transfers between devices, per_device(): lax.psum((local_conv, local_in, local_out), 'rx')  85.6 us
    dot_general x64, matrix products, matrix_step(): jnp.einsum('snm,smk->snk', gain_row[:, None, None] * base_matrix[None], p...  53.4 us
  transfers between devices with their start and end apart: 4, of which 3 were waited for; matrix products, arithmetic and copies ran while one was open for 9% of the time, Pallas kernels for 0%

commit v1 on v0

v1 whole, which is shorter than its diff:
```python
import math

import jax
import jax.numpy as jnp
from jax import lax
from jax.sharding import PartitionSpec as P

BETA = 0.5
HIGH = lax.Precision.HIGHEST
LOG_MUTE = math.log(0.75)
BF = jnp.bfloat16
F32 = jnp.float32


def delay(values, offset):
    if offset == 0:
        return values
    length = values.shape[-1]
    filler = jnp.zeros(values.shape[:-1] + (abs(offset),), values.dtype)
    if offset > 0:
        return jnp.concatenate([values[..., offset:], filler], axis=-1)
    return jnp.concatenate([filler, values[..., : length + offset]], axis=-1)


def high(a, b):
    return jnp.dot(a, b, precision=HIGH)


def low(a, b, dims=((1,), (0,))):
    return lax.dot_general(
        a.astype(BF), b.astype(BF), (dims, ((), ())), preferred_element_type=F32
    )


def powers(first, matrix, count):
    width = first.shape[0]
    rows = first
    have = 1
    while have < count:
        rows = jnp.concatenate([rows, high(rows, matrix)], axis=0)
        matrix = high(matrix, matrix)
        have *= 2
    return rows[: count * width], matrix


def toeplitz(v):
    r, c = v.shape
    w = jnp.concatenate([v, jnp.zeros_like(v)], axis=0)
    flat = jnp.tile(w, (r, 1))[: r * (2 * r - 1)]
    return flat.reshape(r, 2 * r - 1, c)[:, :r]


def untoeplitz(x):
    r, _, c = x.shape
    wide = jnp.concatenate([x, jnp.zeros_like(x)], axis=1)
    flat = wide.reshape(r * 2 * r, c)
    flat = jnp.concatenate([flat, jnp.zeros((r, c), x.dtype)], axis=0)
    return flat.reshape(r, 2 * r + 1, c)[:, :r].sum(axis=0)


def per_device(
    traces, cotangent, mute_mask, dead_flags, first_conv_weights, first_bias, conv_taps,
    in_proj, out_proj, decay_rates, low_rank, mix_weights, back_weights, read_weights,
    down_basis, up_basis,
):
    devices, mine = lax.axis_size("rx"), lax.axis_index("rx")
    nr, _, nt = traces.shape
    taps, nc = first_conv_weights.shape
    nn = in_proj.shape[0]
    nk = down_basis.shape[0]
    cot = cotangent[:, 0].astype(F32)
    u = low_rank * lax.rsqrt(jnp.sum(low_rank * low_rank) + 1e-06)
    matrix = jnp.diag(jnp.exp(-decay_rates)) - BETA * jnp.outer(u, u)
    inp = in_proj.astype(F32)
    outp = out_proj.astype(F32)
    av = high(read_weights, outp)
    bv = high(mix_weights, outp)
    first = jnp.concatenate([inp.T, jnp.eye(nn, dtype=F32)], axis=0)
    rows, shard_power = powers(first, matrix, nr)
    rows = rows.reshape(nr, nc + nn, nn)
    ip, pw = rows[:, :nc], rows[:, nc:]
    nexts = high(pw.reshape(nr * nn, nn), matrix).reshape(nr, nn, nn)
    dev_rows, _ = powers(jnp.eye(nn, dtype=F32), shard_power, devices)
    dev_pw = dev_rows.reshape(devices, nn, nn)
    muted = mute_mask[:, 0].astype(F32)
    order = jnp.arange(nr)
    count = jnp.sum(jnp.where(order[None] <= order[:, None], muted[None], 0.0), axis=1)
    total = jnp.sum(muted)
    lead = jnp.exp(LOG_MUTE * count)
    ratio = jnp.where(
        order[None] >= order[:, None],
        jnp.exp(LOG_MUTE * jnp.maximum(count[None, :] - count[:, None], 0.0)), 0.0,
    )
    tail = jnp.exp(LOG_MUTE * (total - count))
    wa = high(nexts.reshape(nr * nn, nn), av).reshape(nr, nn) * lead[:, None]
    wb = high(nexts.reshape(nr * nn, nn), bv).reshape(nr, nn) * lead[:, None]
    ka = toeplitz(jnp.einsum("qcn,n->qc", ip, av, precision=HIGH)) * ratio[:, :, None]
    kb = toeplitz(jnp.einsum("qcn,n->qc", ip, bv, precision=HIGH)) * ratio[:, :, None]
    kend = ip[::-1].swapaxes(1, 2) * tail[:, None, None]
    kmat = jnp.concatenate([kb, ka, kend], axis=1).astype(BF)
    q_local = low(wa, cot, ((0,), (0,)))
    p_local = low(wb, down_basis, ((0,), (1,)))
    coupling = jnp.sum(read_weights * back_weights)
    spread_grad = (coupling * cot).astype(BF)
    early = jnp.concatenate([p_local, q_local], axis=1).astype(BF)
    early = lax.all_gather(early, "rx")
    totals = lax.all_gather(total, "rx")
    partial_grad = low(up_basis, spread_grad, ((0,), (0,)))
    places = jnp.arange(devices)
    upto = jnp.sum(jnp.where(places[None] <= places[:, None], totals[None], 0.0), axis=1)
    reached = jnp.sum(jnp.where(places <= mine, totals, 0.0))
    entered = jnp.sum(jnp.where(places < mine, totals, 0.0))
    before = upto - totals
    later_gain = jnp.where(
        places > mine, jnp.exp(LOG_MUTE * jnp.maximum(before - reached, 0.0)), 0.0
    )
    earlier_gain = jnp.where(
        places < mine, jnp.exp(LOG_MUTE * jnp.maximum(entered - upto, 0.0)), 0.0
    )
    doubled = jnp.concatenate([dev_pw, dev_pw], axis=0)
    later_pw = lax.dynamic_slice_in_dim(
        doubled, devices - 1 - mine, devices, axis=0
    )
    reverse = doubled[::-1]
    earlier_pw = lax.dynamic_slice_in_dim(
        reverse, 2 * devices - 1 - (devices + mine - 1), devices, axis=0
    )
    later_w = (later_pw * later_gain[:, None, None]).transpose(1, 0, 2).reshape(nn, -1)
    earlier_w = (earlier_pw * earlier_gain[:, None, None]).transpose(1, 0, 2).reshape(nn, -1)
    pq = low(later_w, early.reshape(devices * nn, -1))
    p_mine, q_mine = pq[:, :nk], pq[:, nk:]
    signal = traces[:, 0].astype(F32) * (1.0 - dead_flags.astype(F32))[:, None]
    pre_one = first_bias[None, :, None]
    for j in range(taps):
        pre_one = pre_one + first_conv_weights[j][None, :, None] * delay(signal, j - 1)[:, None]
    h1 = (0.5 * pre_one * (1.0 + jnp.tanh(0.5 * pre_one))).astype(BF)
    h1s = jnp.concatenate([delay(h1, (j - 1) * 4) for j in range(taps)], axis=1)
    wide_taps = conv_taps.transpose(1, 0, 2).reshape(nc, taps * nc)
    pre_two = jnp.einsum("dx,rxt->rdt", wide_taps, h1s, preferred_element_type=F32)
    h2 = (h1.astype(F32) + 0.5 * pre_two * (1.0 + jnp.tanh(0.5 * pre_two))).astype(BF)
    direct_mix = jnp.einsum("c,rct->rt", mix_weights.astype(BF), h2, preferred_element_type=F32)
    direct_read = jnp.einsum("c,rct->rt", read_weights, h2.astype(F32), precision=HIGH)
    z = low(
        kmat.transpose(1, 0, 2).reshape(-1, nr * nc), h2.reshape(nr * nc, nt)
    )
    z = z - jnp.mean(z, axis=-1, keepdims=True)
    s_local = z[:nr] + direct_mix
    pred_local = z[nr : 2 * nr] + direct_read
    end = z[2 * nr :]
    partial = low(down_basis, s_local) + low(p_mine, end, ((0,), (0,)))
    both = lax.psum_scatter(
        jnp.concatenate(
            [partial.reshape(devices, -1, nt), partial_grad.reshape(devices, -1, nt)], axis=1
        ).reshape(-1, nt).astype(BF),
        "rx", scatter_dimension=0, tiled=True,
    ).astype(F32)
    ends = lax.all_gather(end.astype(BF), "rx")
    share = nk // devices
    act = jnp.tanh(both[:share])
    bg = both[share:] * (1.0 - act * act)
    shared = lax.all_gather(jnp.stack([act, bg]).astype(BF), "rx")
    active = shared[:, 0].reshape(nk, nt)
    bottle_grad = shared[:, 1].reshape(nk, nt)
    entering = low(earlier_w, ends.reshape(devices * nn, nt))
    summary = s_local + low(wb, entering)
    predicted = pred_local + low(wa, entering) + coupling * low(up_basis, active)
    grad_up = low(spread_grad, active, ((1,), (1,)))
    grad_down = low(bottle_grad, summary, ((1,), (1,)))
    sg = low(down_basis, bottle_grad, ((0,), (0,)))
    arriving = q_mine + low(p_mine, bottle_grad)
    s = jnp.concatenate([sg, cot, arriving], axis=0)
    s = s.astype(BF)
    s_total = jnp.sum(s.astype(F32), axis=-1)
    h2_mean = jnp.mean(h2.astype(F32), axis=-1)
    back = jnp.einsum("qjc,jt->qct", kmat, s, preferred_element_type=F32)
    back = back - jnp.mean(back, axis=-1, keepdims=True)
    mixed_grad = (
        read_weights[None, :, None] * cot[:, None] + mix_weights[None, :, None] * sg[:, None]
    )
    sig = 0.5 * (1.0 + jnp.tanh(0.5 * pre_two))
    pre_grad = ((mixed_grad + back) * (sig * (1.0 + pre_two * (1.0 - sig)))).astype(BF)
    local_conv = jnp.einsum("rdt,rxt->dx", pre_grad, h1s, preferred_element_type=F32)
    local_conv = local_conv.reshape(nc, taps, nc).transpose(1, 0, 2)
    f = jnp.einsum("jt,qct->qjc", s, h2, preferred_element_type=F32)
    f = f - s_total[None, :, None] * h2_mean[:, None, :]
    f_sg = untoeplitz(f[:, :nr] * ratio[:, :, None])
    f_cot = untoeplitz(f[:, nr : 2 * nr] * ratio[:, :, None])
    f_end = f[:, 2 * nr :] * tail[:, None, None]
    ma = high(pw.reshape(nr * nn, nn), av).reshape(nr, nn)
    mb = high(pw.reshape(nr * nn, nn), bv).reshape(nr, nn)
    local_in = (
        low(ma, f_cot, ((0,), (0,)))
        + low(mb, f_sg, ((0,), (0,)))
        + jnp.einsum("qnm,qmc->nc", pw[::-1].astype(BF), f_end.astype(BF),
                     preferred_element_type=F32)
    )
    z_cot = low(cot, entering, ((1,), (1,))) * lead[:, None]
    z_sg = low(sg, entering, ((1,), (1,))) * lead[:, None]
    x = jnp.stack(
        [
            jnp.einsum("qcn,qc->n", ip, ff, precision=HIGH)
            + jnp.einsum("qnm,qm->n", nexts, zz, precision=HIGH)
            for ff, zz in ((f_cot, z_cot), (f_sg, z_sg))
        ]
    )
    grad_conv, grad_in, x = lax.psum((local_conv, local_in, x), "rx")
    grad_out = read_weights[:, None] * x[0][None] + mix_weights[:, None] * x[1][None]
    return (predicted[:, None], grad_conv, grad_in, grad_out, grad_down, grad_up)


def solution(mesh):
    return jax.shard_map(
        per_device,
        mesh=mesh,
        in_specs=(
            P("rx", "group", None), P("rx", "group", None), P("rx", "group"), P("rx"),
            P(), P(), P(), P(), P(), P(), P(), P(), P(), P(), P(None, "rx"), P("rx", None),
        ),
        out_specs=(
            P("rx", "group", None), P("group", None, None), P("group", None),
            P("group", None), P("group", "rx"), P("rx", "group"),
        ),
        check_vma=False,
    )
```

time: 1270 us -> 453 us (0.36)
  other arithmetic: 523 us -> 37.9 us
  matrix products: 265 us -> 105 us
  local copies, waits for them, and re-layouts: 211 us -> 107 us
  waiting for transfers between devices: 184 us -> 121 us
    dynamic_update_slice x128 -> x0, other arithmetic: 245 us -> none  [per_device(): final_state, states = lax.scan(forward_step, entering[1], (drive, gains))]
    dynamic_slice x320 -> x0, local copies, waits for them, and re-layouts: 189 us -> none  [per_device(): through, partials = lax.scan(matrix_step, identity_mats, gains)]
    dot_general x373 -> x57, matrix products: 265 us -> 105 us  [the longest x26 26.3 us: high(): return jnp.dot(a, b, precision=HIGH)]
    mul x386 -> x5, other arithmetic: 153 us -> 6.27 us  [the longest x1 2.08 us: per_device(): f_sg = untoeplitz(f[:, :nr] * ratio[:, :, None])]
    add x64 -> x1, other arithmetic: 105 us -> 0.7 us  [per_device(): read_weights[:, None] * x[0][None] + mix_weights[:, None] * x[1][None]]
    psum x2 -> x1, waiting for transfers between devices: 176 us -> 83.3 us  [per_device(): grad_conv, grad_in, x = lax.psum((local_conv, local_in, x), 'rx')]
    reshape x0 -> x11, local copies, waits for them, and re-layouts: none -> 41.9 us  [the longest x2 15.3 us: untoeplitz(): return flat.reshape(r, 2 * r + 1, c)[:, :r].sum(axis=0)]
    reduce_scatter x0 -> x1, waiting for transfers between devices: none -> 38.2 us  [per_device(): lax.psum_scatter(jnp.concatenate([partial.reshape(devices, -1, nt), parti...]
  transfers between devices with their start and end apart: 4 -> 4, of which waited for: 3 -> 2; matrix products, arithmetic and copies ran while one was open for 9% -> 30% of each run, Pallas kernels for 0% -> 0%
where the time goes in v1:
time: 453 us; the launch traced here: 444 us
  waiting for transfers between devices  121 us (27%)
  local copies, waits for them, and re-layouts  107 us (24%)
  matrix products  105 us (23%)
  blocking collectives  56.2 us (12%)
  other arithmetic  37.9 us (8%)
  between operations  15.9 us (4%)
    psum x1, waiting for transfers between devices, per_device(): grad_conv, grad_in, x = lax.psum((local_conv, local_in, x), 'rx')  83.3 us
    reduce_scatter x1, waiting for transfers between devices, per_device(): lax.psum_scatter(jnp.concatenate([partial.reshape(devices, -1, nt), parti...  38.2 us
    unnamed x1, blocking collectives  35.2 us
    dot_general x26, matrix products, high(): return jnp.dot(a, b, precision=HIGH)  26.3 us
    dot_general x18, matrix products, low(): lax.dot_general(a.astype(BF), b.astype(BF), (dims, ((), ())), preferred_e...  22.6 us
    unnamed x140, local copies, waits for them, and re-layouts  22 us
    all_gather x1, blocking collectives, per_device(): shared = lax.all_gather(jnp.stack([act, bg]).astype(BF), 'rx')  21.1 us
    reshape x2, local copies, waits for them, and re-layouts, untoeplitz(): return flat.reshape(r, 2 * r + 1, c)[:, :r].sum(axis=0)  15.3 us
  transfers between devices with their start and end apart: 4, of which 2 were waited for; matrix products, arithmetic and copies ran while one was open for 30% of the time, Pallas kernels for 0%

profile of v1, /device:TPU:0, one launch (start us, length us, event | category | flops | bytes accessed | tf_op | source)
XLA Modules:
  0.0 443.7 jit_solution(2840967292673099368)
XLA Ops:
  19.2 2.1 fusion.185
  21.3 2.5 concatenate.119
  24.1 2.1 fusion.172
  27.9 2.3 fusion.94
  35.5 2.4 copy.105
  37.8 5.0 %fusion.129 = f32[1,64,64]{2,0,1:T(1,128)S(1)} fusion(f32[64,64,64]{2,1,0:T(8,128)S(1)} %copy.105, f32[1,64]{1,0:T(1,128)S(1)} %copy-done.47), kind=kOutput, calls=%fused_computation.203 | convolution fusion | flops 3145728 | bytes 1065216 | tf_op jit(solution)/shard_map/qcn,n->qc/dot_general | solution.py:97
  42.8 5.6 %fusion.133 = f32[1,64,64]{2,0,1:T(1,128)S(1)} fusion(f32[64,64,64]{2,1,0:T(8,128)S(1)} %copy.105, f32[1,64]{1,0:T(1,128)} %copy-done.45), kind=kOutput, calls=%fused_computation.207 | convolution fusion | flops 3145728 | bytes 1065216 | tf_op jit(solution)/shard_map/qcn,n->qc/dot_general | solution.py:98
  55.1 2.5 copy.124
  57.7 6.4 %reshape.260 = f32[64,127,64]{1,0,2:T(8,128)} reshape(f32[8128,64]{0,1:T(8,128)} %bitcast.318) | data formatting | bytes 4161536 | tf_op jit(solution)/shard_map/reshape | solution.py:50
  64.0 3.4 copy.106
  67.5 2.5 copy.123
  70.1 6.8 %reshape.261 = f32[64,127,64]{1,0,2:T(8,128)} reshape(f32[8128,64]{0,1:T(8,128)} %bitcast.321) | data formatting | bytes 4161536 | tf_op jit(solution)/shard_map/reshape | solution.py:50
  76.8 3.3 copy.107
  80.2 3.7 multiply_convert_fusion.3
  83.8 2.3 copy.73
  86.1 2.3 copy.74
  88.4 4.2 multiply_convert_fusion
  92.7 2.6 fusion.171
  95.4 9.5 %convert_reduce_fusion = (f32[64,64]{1,0:T(8,128)}, bf16[64,64,512]{2,1,0:T(8,128)(2,1)S(1)}, f32[64,512,64]{1,2,0:T(8,128)}) fusion(f32[64,512]{1,0:T(8,128)S(1)} %copy-done.27, f32[64]{0:T(128)S(1)} %copy-done.56, f32[64,512]{1,0:T(8,128)S(1)} %copy-done.25, f32[64]{0:T(128)S(1)} %copy-done.57, f32[64,512]{1,0:T(8,128)S(1)} %copy-done.26, ...), kind=kOutput, calls=%fused_computation.12 | convolution fusion | flops 905965568 | bytes 25535488 | tf_op jit(solution)/shard_map/dx,rxt->rdt/dot_general | solution.py:139
  109.7 3.4 copy.93
  115.1 35.2 %all-reduce.10 = f32[16]{0:T(128)S(1)} all-reduce(f32[16]{0:T(128)S(1)} %dynamic-update-slice), channel_id=1, replica_groups=mesh['group'=2,'rx'=16] {'rx'}, use_global_device_ids=true, to_apply=%add.10 | all-reduce | flops 16 | bytes 128
  156.2 7.2 %fusion.127 = f32[1,64,64]{2,0,1:T(1,128)} fusion(f32[64,64,64]{2,1,0:T(8,128)} %copy.93, f32[1,64]{1,0:T(1,128)} %copy-done.46), kind=kOutput, calls=%fused_computation.201 | convolution fusion | flops 3145728 | bytes 1065216 | tf_op jit(solution)/shard_map/dot_general | solution.py:26
  164.8 2.7 convolution_convert_fusion
  167.4 2.4 compare_select_fusion.1
  169.9 7.2 %fusion.131 = f32[1,64,64]{2,0,1:T(1,128)} fusion(f32[64,64,64]{2,1,0:T(8,128)} %copy.93, f32[1,64]{1,0:T(1,128)} %copy-done.45), kind=kOutput, calls=%fused_computation.205 | convolution fusion | flops 3145728 | bytes 1065216 | tf_op jit(solution)/shard_map/dot_general | solution.py:26
  177.0 2.8 fusion.137
  181.7 2.1 convolution_bitcast_fusion.1
  187.7 2.3 pad_maximum_fusion.1
  190.0 3.6 rev.11
  193.7 2.2 reshape.274
  195.9 2.4 rev.10
  202.7 38.2 %reduce-scatter.2.cloned.1.call-done = bf16[32,512]{1,0:T(8,128)(2,1)} async-done(((bf16[512,512]{1,0:T(8,128)(2,1)}), bf16[32,512]{1,0:T(8,128)(2,1)}) %reduce-scatter.2.cloned.1.call-update) | async-done | bytes 32784 | tf_op jit(solution)/shard_map/reduce_scatter | solution.py:151
  241.7 21.1 %all_gather.25 = bf16[16,2,16,512]{3,2,1,0:T(8,128)(2,1)S(1)} all-gather(bf16[1,2,16,512]{3,2,1,0:T(8,128)(2,1)S(1)} %pad_maximum_fusion.7), channel_id=1, replica_groups=mesh['group'=2,'rx'=16] {'rx'}, dimensions={0}, use_global_device_ids=true | all-gather | bytes 557056 | tf_op jit(solution)/shard_map/all_gather | solution.py:161
  268.6 7.1 %fusion.177 = (f32[64,64]{1,0:T(8,128)}, f32[64,64,512]{2,1,0:T(8,128)}) fusion(bf16[64,512]{1,0:T(8,128)(2,1)S(1)} %fusion.21, bf16[64,512]{1,0:T(8,128)(2,1)S(1)} %bitcast.329, bf16[64,512]{1,0:T(8,128)(2,1)S(1)} %get-tuple-element.64, bf16[64,64,64]{1,2,0:T(8,128)(2,1)S(1)} %copy-done.9, bf16[64,64,64]{1,2,0:T(8,128)(2,1)} %copy.74, ...), kind=kOutput, calls=%fused_computation.264 | convolution fusion | flops 812707840 | bytes 10174464 | tf_op jit(solution)/shard_map/qjc,jt->qct/dot_general | solution.py:175
  277.9 3.7 bitcast_subtract_fusion
  281.5 2.1 slice_multiply_fusion.1
  283.6 2.4 concatenate.140
  286.0 3.8 copy.82
  289.8 3.1 concatenate.141
  292.9 7.5 %reshape.273 = f32[64,129,64]{1,0,2:T(8,128)} reshape(f32[8256,64]{0,1:T(8,128)} %concatenate.141) | data formatting | bytes 4227072 | tf_op jit(solution)/shard_map/reshape | solution.py:58
  303.6 4.2 concatenate.138
  307.8 3.8 copy.81
  311.6 3.1 concatenate.139
  314.6 7.8 %reshape.271 = f32[64,129,64]{1,0,2:T(8,128)} reshape(f32[8256,64]{0,1:T(8,128)} %concatenate.139) | data formatting | bytes 4227072 | tf_op jit(solution)/shard_map/reshape | solution.py:58
  327.9 2.4 convolution_bitcast_fusion.4
  330.4 2.8 fusion.30
  335.9 11.5 %fusion.8 = f32[64,192,1]{0,1,2:T(8,128)} fusion(f32[64,512,64]{1,2,0:T(8,128)} %get-tuple-element.61, f32[64,64,512]{2,1,0:T(8,128)} %get-tuple-element.67, f32[64,64]{1,0:T(8,128)S(1)} %broadcast_multiply_fusion.1, f32[64,512]{1,0:T(8,128)S(1)} %copy-done.38, f32[64]{0:T(128)S(1)} %copy-done.53, f32[64,512]{1,0:T(8,128)S(1)} %copy-done.37, ...), kind=kOutput, calls=%fused_computation.17 | convolution fusion | flops 897581056 | bytes 29622784 | tf_op jit(solution)/shard_map/rdt,rxt->dx/dot_general | solution.py:182
  349.1 83.3 %all-reduce.14.cloned.1.call-done = (f32[3,64,64]{1,2,0:T(8,128)}, f32[64,64]{1,0:T(8,128)}, f32[2,64]{1,0:T(2,128)}) async-done(((f32[3,64,64]{1,2,0:T(8,128)}, f32[64,64]{1,0:T(8,128)}, f32[2,64]{1,0:T(2,128)}), (f32[3,64,64]{1,2,0:T(8,128)}, f32[64,64]{1,0:T(8,128)}, f32[2,64]{1,0:T(2,128)})) %all-reduce.14.cloned.1.call-update) | async-done | bytes 66064 | tf_op jit(solution)/shard_map/psum | solution.py:206
  (248 shorter events, 75.5 us)
Async XLA Ops:
  7.2 24.5 %copy-start = (bf16[256,64]{0,1:T(8,128)(2,1)S(1)}, bf16[256,64]{0,1:T(8,128)(2,1)}, u32[]{:S(2)}) copy-start(bf16[256,64]{0,1:T(8,128)(2,1)} %param.30) | copy-start | bytes 98308
  7.2 174.5 %all-gather.4.cloned.1.call-start = ((), (), s32[]{:S(2)}) async-start(), calls=%async_computation.1 | async-start | bytes 1671168 | tf_op jit(solution)/shard_map/all_gather | solution.py:106
  12.0 18.9 %copy-start.46 = (f32[1,64]{1,0:T(1,128)}, f32[1,64]{1,0:T(1,128)S(1)}, u32[]{:S(2)}) copy-start(f32[1,64]{1,0:T(1,128)S(1)} %fusion.143) | copy-start | bytes 772
  12.9 17.3 %copy-start.45 = (f32[1,64]{1,0:T(1,128)}, f32[1,64]{1,0:T(1,128)S(1)}, u32[]{:S(2)}) copy-start(f32[1,64]{1,0:T(1,128)S(1)} %fusion.145) | copy-start | bytes 772
  17.2 14.5 %copy-start.42 = (f32[64]{0:T(128)}, f32[64]{0:T(128)S(1)}, u32[]{:S(2)}) copy-start(f32[64]{0:T(128)S(1)} %get-tuple-element.59) | copy-start | bytes 772
  26.2 9.2 %copy-start.4 = (f32[64,64,64]{1,0,2:T(8,128)}, f32[64,64,64]{1,0,2:T(8,128)S(1)}, u32[]{:S(2)}) copy-start(f32[64,64,64]{1,0,2:T(8,128)S(1)} %get-tuple-element.42) | copy-start | bytes 3145732
  30.9 11.9 %copy-start.30 = (f32[64,64]{1,0:T(8,128)}, f32[64,64]{1,0:T(8,128)S(1)}, u32[]{:S(2)}) copy-start(f32[64,64]{1,0:T(8,128)S(1)} %reshape.266) | copy-start | bytes 49156
  32.8 165.6 %all-gather.6.cloned.1.call-start = ((), (), s32[]{:S(2)}) async-start(), calls=%async_computation.3 | async-start | bytes 1114112 | tf_op jit(solution)/shard_map/all_gather | solution.py:157
  37.8 10.6 %copy-start.59 = (f32[3,64]{1,0:T(4,128)S(1)}, f32[3,64]{1,0:T(4,128)}, u32[]{:S(2)}) copy-start(f32[3,64]{1,0:T(4,128)} %param.20) | copy-start | bytes 2308
  49.9 30.3 %copy-start.28 = (f32[64,64]{1,0:T(8,128)}, f32[64,64]{1,0:T(8,128)S(1)}, u32[]{:S(2)}) copy-start(f32[64,64]{1,0:T(8,128)S(1)} %copy.71) | copy-start | bytes 49156
  80.1 8.3 %copy-start.25 = (f32[64,512]{1,0:T(8,128)S(1)}, f32[64,512]{1,0:T(8,128)}, u32[]{:S(2)}) copy-start(f32[64,512]{1,0:T(8,128)} %fusion.50) | copy-start | bytes 393220
  80.1 8.3 %copy-start.55 = (f32[64]{0:T(128)S(1)}, f32[64]{0:T(128)}, u32[]{:S(2)}) copy-start(f32[64]{0:T(128)} %get-tuple-element.52) | copy-start | bytes 772
  80.1 8.3 %copy-start.56 = (f32[64]{0:T(128)S(1)}, f32[64]{0:T(128)}, u32[]{:S(2)}) copy-start(f32[64]{0:T(128)} %get-tuple-element.53) | copy-start | bytes 772
  80.2 8.2 %copy-start.57 = (f32[64]{0:T(128)S(1)}, f32[64]{0:T(128)}, u32[]{:S(2)}) copy-start(f32[64]{0:T(128)} %get-tuple-element.54) | copy-start | bytes 772
  80.2 8.2 %copy-start.60 = (f32[64]{0:T(128)S(1)}, f32[64]{0:T(128)}, u32[]{:S(2)}) copy-start(f32[64]{0:T(128)} %param.21) | copy-start | bytes 772
  95.3 9.6 %copy-start.12 = (bf16[64,64,508]{2,1,0:T(8,128)(2,1)}, bf16[64,64,508]{2,1,0:T(8,128)(2,1)S(1)}, u32[]{:S(2)}) copy-start(bf16[64,64,508]{2,1,0:T(8,128)(2,1)S(1)} %get-tuple-element.40) | copy-start | bytes 12484612
  95.3 9.5 %copy-start.13 = (bf16[64,64,508]{2,1,0:T(8,128)(2,1)}, bf16[64,64,508]{2,1,0:T(8,128)(2,1)S(1)}, u32[]{:S(2)}) copy-start(bf16[64,64,508]{2,1,0:T(8,128)(2,1)S(1)} %get-tuple-element.41) | copy-start | bytes 12484612
  95.4 9.5 %copy-start.8 = (bf16[64,64,64]{1,2,0:T(8,128)(2,1)S(1)}, bf16[64,64,64]{1,2,0:T(8,128)(2,1)}, u32[]{:S(2)}) copy-start(bf16[64,64,64]{1,2,0:T(8,128)(2,1)} %fusion.33) | copy-start | bytes 1572868
  95.4 9.5 %copy-start.10 = (bf16[64,64,64]{1,2,0:T(8,128)(2,1)S(1)}, bf16[64,64,64]{1,2,0:T(8,128)(2,1)}, u32[]{:S(2)}) copy-start(bf16[64,64,64]{1,2,0:T(8,128)(2,1)} %copy.73) | copy-start | bytes 1572868
  95.4 9.5 %copy-start.11 = (bf16[64,64,64]{1,2,0:T(8,128)(2,1)S(1)}, bf16[64,64,64]{1,2,0:T(8,128)(2,1)}, u32[]{:S(2)}) copy-start(bf16[64,64,64]{1,2,0:T(8,128)(2,1)} %copy.74) | copy-start | bytes 1572868
  106.9 44.7 %copy-start.49 = (f32[64]{0:T(128)S(1)}, f32[64]{0:T(128)}, u32[]{:S(2)}) copy-start(f32[64]{0:T(128)} %param.29) | copy-start | bytes 772
  106.9 44.7 %copy-start.62 = (f32[64]{0:T(128)S(1)}, f32[64]{0:T(128)}, u32[]{:S(2)}) copy-start(f32[64]{0:T(128)} %param.28) | copy-start | bytes 772
  108.4 132.5 %reduce-scatter.2.cloned.1.call-start = ((), (), s32[]{:S(2)}) async-start(), calls=%async_computation.2 | async-start | bytes 557056 | tf_op jit(solution)/shard_map/reduce_scatter | solution.py:151
  154.2 22.8 %copy-start.52 = (f32[64]{0:T(128)S(1)}, f32[64]{0:T(128)}, u32[]{:S(2)}) copy-start(f32[64]{0:T(128)} %param.27) | copy-start | bytes 772
  156.2 23.7 %copy-start.50 = (f32[64]{0:T(128)S(1)}, f32[64]{0:T(128)}, u32[]{:S(2)}) copy-start(f32[64]{0:T(128)} %param.29) | copy-start | bytes 772
  164.8 15.1 %copy-start.7 = (bf16[64,64,512]{2,1,0:T(8,128)(2,1)S(1)}, bf16[64,64,512]{2,1,0:T(8,128)(2,1)}, u32[]{:S(2)}) copy-start(bf16[64,64,512]{2,1,0:T(8,128)(2,1)} %copy-done.6) | copy-start | bytes 12582916
  187.7 244.6 %all-reduce.14.cloned.1.call-start = ((), (), s32[]{:S(2)}) async-start(), calls=%async_computation.4 | async-start | bytes 264192 | tf_op jit(solution)/shard_map/psum | solution.py:206
  190.0 8.3 %copy-start.54 = (f32[16]{0:T(128)S(1)}, f32[16]{0:T(128)}, u32[]{:S(2)}) copy-start(f32[16]{0:T(128)} %get-tuple-element.58) | copy-start | bytes 196
  193.7 69.8 %copy-start.31 = (f32[64,64]{1,0:T(8,128)S(1)}, f32[64,64]{1,0:T(8,128)}, u32[]{:S(2)}) copy-start(f32[64,64]{1,0:T(8,128)} %copy-done.30) | copy-start | bytes 49156
  193.7 69.8 %copy-start.44 = (f32[64]{0:T(128)S(1)}, f32[64]{0:T(128)}, u32[]{:S(2)}) copy-start(f32[64]{0:T(128)} %copy-done.42) | copy-start | bytes 772
  195.9 72.7 %copy-start.9 = (bf16[64,64,64]{1,2,0:T(8,128)(2,1)S(1)}, bf16[64,64,64]{1,2,0:T(8,128)(2,1)}, u32[]{:S(2)}) copy-start(bf16[64,64,64]{1,2,0:T(8,128)(2,1)} %fusion.33) | copy-start | bytes 1572868
  200.2 41.5 %copy-start.17 = (bf16[64,512]{1,0:T(8,128)(2,1)}, bf16[64,512]{1,0:T(8,128)(2,1)S(1)}, u32[]{:S(2)}) copy-start(bf16[64,512]{1,0:T(8,128)(2,1)S(1)} %fusion.22) | copy-start | bytes 196612
  266.6 9.1 %copy-start.22 = (bf16[64,512]{1,0:T(8,128)(2,1)}, bf16[64,512]{1,0:T(8,128)(2,1)S(1)}, u32[]{:S(2)}) copy-start(bf16[64,512]{1,0:T(8,128)(2,1)S(1)} %fusion.21) | copy-start | bytes 196612
  267.4 8.3 %copy-start.19 = (bf16[64,512]{1,0:T(8,128)(2,1)}, bf16[64,512]{1,0:T(8,128)(2,1)S(1)}, u32[]{:S(2)}) copy-start(bf16[64,512]{1,0:T(8,128)(2,1)S(1)} %get-tuple-element.64) | copy-start | bytes 196612
  268.6 9.3 %copy-start.41 = (f32[64,64]{1,0:T(8,128)S(1)}, f32[64,64]{1,0:T(8,128)}, u32[]{:S(2)}) copy-start(f32[64,64]{1,0:T(8,128)} %broadcast_multiply_fusion) | copy-start | bytes 49156
  314.6 9.7 %copy-start.34 = (f32[1,64,64]{2,0,1:T(1,128)S(1)}, f32[1,64,64]{2,0,1:T(1,128)}, u32[]{:S(2)}) copy-start(f32[1,64,64]{2,0,1:T(1,128)} %fusion.127) | copy-start | bytes 49156
  314.6 13.3 %copy-start.20 = (bf16[64,64,64]{1,0,2:T(8,128)(2,1)S(1)}, bf16[64,64,64]{1,0,2:T(8,128)(2,1)}, u32[]{:S(2)}) copy-start(bf16[64,64,64]{1,0,2:T(8,128)(2,1)} %rev.11) | copy-start | bytes 1572868
  322.4 10.7 %copy-start.35 = (f32[64,64]{1,0:T(8,128)S(1)}, f32[64,64]{1,0:T(8,128)}, u32[]{:S(2)}) copy-start(f32[64,64]{1,0:T(8,128)} %convolution_multiply_fusion.2) | copy-start | bytes 49156
  325.3 9.8 %copy-start.33 = (f32[1,64,64]{2,0,1:T(1,128)S(1)}, f32[1,64,64]{2,0,1:T(1,128)}, u32[]{:S(2)}) copy-start(f32[1,64,64]{2,0,1:T(1,128)} %fusion.131) | copy-start | bytes 49156
  325.3 9.8 %copy-start.36 = (f32[64,64]{1,0:T(8,128)S(1)}, f32[64,64]{1,0:T(8,128)}, u32[]{:S(2)}) copy-start(f32[64,64]{1,0:T(8,128)} %fusion.103) | copy-start | bytes 49156
  325.3 10.5 %copy-start.3 = (bf16[64,64,512]{2,1,0:T(8,128)(2,1)S(1)}, bf16[64,64,512]{2,1,0:T(8,128)(2,1)}, u32[]{:S(2)}) copy-start(bf16[64,64,512]{2,1,0:T(8,128)(2,1)} %copy-done.2) | copy-start | bytes 12582916
  325.3 10.5 %copy-start.37 = (f32[64,512]{1,0:T(8,128)S(1)}, f32[64,512]{1,0:T(8,128)}, u32[]{:S(2)}) copy-start(f32[64,512]{1,0:T(8,128)} %convert_bitcast_fusion.1) | copy-start | bytes 393220
  325.3 10.5 %copy-start.38 = (f32[64,512]{1,0:T(8,128)S(1)}, f32[64,512]{1,0:T(8,128)}, u32[]{:S(2)}) copy-start(f32[64,512]{1,0:T(8,128)} %get-tuple-element.65) | copy-start | bytes 393220
  325.3 10.5 %copy-start.51 = (f32[64]{0:T(128)S(1)}, f32[64]{0:T(128)}, u32[]{:S(2)}) copy-start(f32[64]{0:T(128)} %param.29) | copy-start | bytes 772
  325.3 10.5 %copy-start.53 = (f32[64]{0:T(128)S(1)}, f32[64]{0:T(128)}, u32[]{:S(2)}) copy-start(f32[64]{0:T(128)} %param.27) | copy-start | bytes 772
  335.9 11.6 %copy-start.24 = (f32[64,512]{1,0:T(8,128)S(1)}, f32[64,512]{1,0:T(8,128)}, u32[]{:S(2)}) copy-start(f32[64,512]{1,0:T(8,128)} %convolution_add_fusion.2) | copy-start | bytes 393220
  335.9 11.6 %copy-start.39 = (bf16[64,256]{1,0:T(8,128)(2,1)S(1)}, bf16[64,256]{1,0:T(8,128)(2,1)}, u32[]{:S(2)}) copy-start(bf16[64,256]{1,0:T(8,128)(2,1)} %param.31) | copy-start | bytes 98308
  335.9 100.9 %copy-start.1 = (bf16[256,64]{0,1:T(8,128)(2,1)S(1)}, bf16[256,64]{0,1:T(8,128)(2,1)}, u32[]{:S(2)}) copy-start(bf16[256,64]{0,1:T(8,128)(2,1)} %param.30) | copy-start | bytes 98308
  (20 other events, 89.1 us)
Sparse Core Ops, SparseCore 0:
  32.9 42.3 all-gather.3
  108.6 40.8 all-gather.5
  187.8 53.0 reduce-scatter.1
  347.6 84.7 all-reduce.13

commit v2 on v1

--- a/solution.py
+++ b/solution.py
@@ -1,8 +1,11 @@
+import functools
 import math
 
 import jax
 import jax.numpy as jnp
 from jax import lax
+from jax.experimental import pallas as pl
+from jax.experimental.pallas import tpu as pltpu
 from jax.sharding import PartitionSpec as P
 
 BETA = 0.5
@@ -10,6 +13,7 @@
 LOG_MUTE = math.log(0.75)
 BF = jnp.bfloat16
 F32 = jnp.float32
+MESH = pl.DeviceIdType.MESH
 
 
 def delay(values, offset):
@@ -43,19 +47,123 @@
     return rows[: count * width], matrix
 
 
-def toeplitz(v):
-    r, c = v.shape
-    w = jnp.concatenate([v, jnp.zeros_like(v)], axis=0)
-    flat = jnp.tile(w, (r, 1))[: r * (2 * r - 1)]
-    return flat.reshape(r, 2 * r - 1, c)[:, :r]
-
-
-def untoeplitz(x):
-    r, _, c = x.shape
-    wide = jnp.concatenate([x, jnp.zeros_like(x)], axis=1)
-    flat = wide.reshape(r * 2 * r, c)
-    flat = jnp.concatenate([flat, jnp.zeros((r, c), x.dtype)], axis=0)
-    return flat.reshape(r, 2 * r + 1, c)[:, :r].sum(axis=0)
+def gain_from(count_ref, q, order):
+    passed = jnp.maximum(count_ref[...] - count_ref[q : q + 1, :], 0.0)
+    return jnp.where(order >= q, jnp.exp(LOG_MUTE * passed), 0.0)
+
+
+def spread_kernel(v_ref, count_ref, out_ref):
+    v = v_ref[...]
+    order = lax.broadcasted_iota(jnp.int32, v.shape, 0)
+    for q in range(v.shape[0]):
+        moved = pltpu.roll(v, q, 0) if q else v
+        out_ref[q] = (moved * gain_from(count_ref, q, order)).astype(out_ref.dtype)
+
+
+def gather_kernel(x_ref, count_ref, out_ref):
+    nr = x_ref.shape[0]
+    order = lax.broadcasted_iota(jnp.int32, x_ref.shape[1:], 0)
+    total = jnp.zeros(x_ref.shape[1:], F32)
+    for q in range(nr):
+        part = x_ref[q] * gain_from(count_ref, q, order)
+        total = total + (pltpu.roll(part, nr - q, 0) if q else part)
+    out_ref[...] = total
+
+
+def whole_call(kernel, out_shape, *operands):
+    return pl.pallas_call(
+        kernel,
+        out_shape=out_shape,
+        compiler_params=pltpu.CompilerParams(vmem_limit_bytes=40 << 20),
+    )(*operands)
+
+
+def meet(devices):
+    me = lax.axis_index("rx")
+    barrier = pltpu.get_barrier_semaphore()
+
+    def greet(i, c):
+        pl.semaphore_signal(
+            barrier, inc=1, device_id={"rx": lax.rem(me + i, devices)}, device_id_type=MESH
+        )
+        return c
+
+    lax.fori_loop(1, devices, greet, 0)
+    pl.semaphore_wait(barrier, devices - 1)
+    return me
+
+
+def sends(devices, me, pick, sems):
+    def copy(i):
+        peer = lax.rem(me + i, devices)
+        src, dst = pick(peer)
+        return pltpu.make_async_remote_copy(
+            src_ref=src, dst_ref=dst, send_sem=sems[0].at[i], recv_sem=sems[1].at[i],
+            device_id={"rx": peer}, device_id_type=MESH,
+        )
+
+    def start(i, c):
+        copy(i).start()
+        return c
+
+    def wait(i, c):
+        copy(i).wait()
+        return c
+
+    return (
+        lambda: lax.fori_loop(1, devices, start, 0),
+        lambda: lax.fori_loop(1, devices, wait, 0),
+    )
+
+
+def total_of(landed, devices):
+    return lax.fori_loop(
+        1, devices, lambda d, acc: acc + landed[d].astype(F32), landed[0].astype(F32)
+    )
+
+
+def middle_kernel(devices, x_ref, y_ref, shared_ref, ends_ref, landed, s0, r0, s1, r1, s2, r2):
+    me = meet(devices)
+    start, wait = sends(devices, me, lambda p: (x_ref.at[p], landed.at[me]), (s0, r0))
+    start()
+    start_y, wait_y = sends(devices, me, lambda p: (y_ref, ends_ref.at[me]), (s1, r1))
+    start_y()
+    landed[me] = x_ref[me]
+    wait()
+    both = total_of(landed, devices)
+    act = jnp.tanh(both[0])
+    bg = both[1] * (1.0 - act * act)
+    shared_ref[me] = jnp.stack([act, bg]).astype(BF)
+    start, wait = sends(devices, me, lambda p: (shared_ref.at[me], shared_ref.at[me]), (s2, r2))
+    start()
+    ends_ref[me] = y_ref[...]
+    wait_y()
+    wait()
+
+
+def sum_kernel(devices, x_ref, out_ref, landed, s0, r0, s1, r1):
+    me = meet(devices)
+    start, wait = sends(devices, me, lambda p: (x_ref.at[p], landed.at[me]), (s0, r0))
+    start()
+    landed[me] = x_ref[me]
+    wait()
+    out_ref[me] = total_of(landed, devices)
+    start, wait = sends(devices, me, lambda p: (out_ref.at[me], out_ref.at[me]), (s1, r1))
+    start()
+    wait()
+
+
+def remote_call(kernel, devices, ident, pairs, landed, out_shape, *operands):
+    return pl.pallas_call(
+        functools.partial(kernel, devices),
+        out_shape=out_shape,
+        in_specs=[pl.BlockSpec(memory_space=pltpu.VMEM)] * len(operands),
+        out_specs=jax.tree.map(lambda _: pl.BlockSpec(memory_space=pltpu.VMEM), out_shape),
+        scratch_shapes=[landed] + [pltpu.SemaphoreType.DMA((devices,))] * (2 * pairs),
+        compiler_params=pltpu.CompilerParams(
+            collective_id=ident, has_side_effects=True, vmem_limit_bytes=40 << 20
+        ),
+    )(*operands)
 
 
 def per_device(
@@ -87,24 +195,31 @@
     count = jnp.sum(jnp.where(order[None] <= order[:, None], muted[None], 0.0), axis=1)
     total = jnp.sum(muted)
     lead = jnp.exp(LOG_MUTE * count)
-    ratio = jnp.where(
-        order[None] >= order[:, None],
-        jnp.exp(LOG_MUTE * jnp.maximum(count[None, :] - count[:, None], 0.0)), 0.0,
-    )
     tail = jnp.exp(LOG_MUTE * (total - count))
     wa = high(nexts.reshape(nr * nn, nn), av).reshape(nr, nn) * lead[:, None]
     wb = high(nexts.reshape(nr * nn, nn), bv).reshape(nr, nn) * lead[:, None]
-    ka = toeplitz(jnp.einsum("qcn,n->qc", ip, av, precision=HIGH)) * ratio[:, :, None]
-    kb = toeplitz(jnp.einsum("qcn,n->qc", ip, bv, precision=HIGH)) * ratio[:, :, None]
-    kend = ip[::-1].swapaxes(1, 2) * tail[:, None, None]
-    kmat = jnp.concatenate([kb, ka, kend], axis=1).astype(BF)
+    base = jnp.concatenate(
+        [jnp.einsum("qcn,n->qc", ip, v, precision=HIGH) for v in (bv, av)], axis=1
+    )
+    count_wide = jnp.broadcast_to(count[:, None], base.shape)
+    kba = whole_call(
+        spread_kernel, jax.ShapeDtypeStruct((nr, nr, 2 * nc), BF), base, count_wide
+    )
+    kend = (ip[::-1].swapaxes(1, 2) * tail[:, None, None]).astype(BF)
+    kmat = jnp.concatenate([kba[:, :, :nc], kba[:, :, nc:], kend], axis=1)
     q_local = low(wa, cot, ((0,), (0,)))
     p_local = low(wb, down_basis, ((0,), (1,)))
     coupling = jnp.sum(read_weights * back_weights)
     spread_grad = (coupling * cot).astype(BF)
-    early = jnp.concatenate([p_local, q_local], axis=1).astype(BF)
+    coarse = jnp.floor(total / 128.0)
+    lanes = jnp.arange(128)[None]
+    tally = jnp.where(lanes == 0, coarse, jnp.where(lanes == 1, total - 128.0 * coarse, 0.0))
+    early = jnp.concatenate(
+        [p_local, q_local, jnp.broadcast_to(tally, (nn, 128))], axis=1
+    ).astype(BF)
     early = lax.all_gather(early, "rx")
-    totals = lax.all_gather(total, "rx")
+    tallies = early[:, 0, nk + nt :].astype(F32)
+    totals = 128.0 * tallies[:, 0] + tallies[:, 1]
     partial_grad = low(up_basis, spread_grad, ((0,), (0,)))
     places = jnp.arange(devices)
     upto = jnp.sum(jnp.where(places[None] <= places[:, None], totals[None], 0.0), axis=1)
@@ -127,7 +242,7 @@
     )
     later_w = (later_pw * later_gain[:, None, None]).transpose(1, 0, 2).reshape(nn, -1)
     earlier_w = (earlier_pw * earlier_gain[:, None, None]).transpose(1, 0, 2).reshape(nn, -1)
-    pq = low(later_w, early.reshape(devices * nn, -1))
+    pq = low(later_w, early[:, :, : nk + nt].reshape(devices * nn, -1))
     p_mine, q_mine = pq[:, :nk], pq[:, nk:]
     signal = traces[:, 0].astype(F32) * (1.0 - dead_flags.astype(F32))[:, None]
     pre_one = first_bias[None, :, None]
@@ -148,17 +263,17 @@
     pred_local = z[nr : 2 * nr] + direct_read
     end = z[2 * nr :]
     partial = low(down_basis, s_local) + low(p_mine, end, ((0,), (0,)))
-    both = lax.psum_scatter(
-        jnp.concatenate(
-            [partial.reshape(devices, -1, nt), partial_grad.reshape(devices, -1, nt)], axis=1
-        ).reshape(-1, nt).astype(BF),
-        "rx", scatter_dimension=0, tiled=True,
-    ).astype(F32)
-    ends = lax.all_gather(end.astype(BF), "rx")
-    share = nk // devices
-    act = jnp.tanh(both[:share])
-    bg = both[share:] * (1.0 - act * act)
-    shared = lax.all_gather(jnp.stack([act, bg]).astype(BF), "rx")
+    pieces = jnp.stack(
+        [partial.reshape(devices, -1, 128), partial_grad.reshape(devices, -1, 128)], axis=1
+    ).astype(BF)
+    shared, ends = remote_call(
+        middle_kernel, devices, 0, 3, pltpu.VMEM(pieces.shape, BF),
+        (
+            jax.ShapeDtypeStruct(pieces.shape, BF),
+            jax.ShapeDtypeStruct((devices, nn, nt), BF),
+        ),
+        pieces, end.astype(BF),
+    )
     active = shared[:, 0].reshape(nk, nt)
     bottle_grad = shared[:, 1].reshape(nk, nt)
     entering = low(earlier_w, ends.reshape(devices * nn, nt))
@@ -183,8 +298,11 @@
     local_conv = local_conv.reshape(nc, taps, nc).transpose(1, 0, 2)
     f = jnp.einsum("jt,qct->qjc", s, h2, preferred_element_type=F32)
     f = f - s_total[None, :, None] * h2_mean[:, None, :]
-    f_sg = untoeplitz(f[:, :nr] * ratio[:, :, None])
-    f_cot = untoeplitz(f[:, nr : 2 * nr] * ratio[:, :, None])
+    f_both = whole_call(
+        gather_kernel, jax.ShapeDtypeStruct((nr, 2 * nc), F32),
+        jnp.concatenate([f[:, :nr], f[:, nr : 2 * nr]], axis=2), count_wide,
+    )
+    f_sg, f_cot = f_both[:, :nc], f_both[:, nc:]
     f_end = f[:, 2 * nr :] * tail[:, None, None]
     ma = high(pw.reshape(nr * nn, nn), av).reshape(nr, nn)
     mb = high(pw.reshape(nr * nn, nn), bv).reshape(nr, nn)
@@ -203,7 +321,17 @@
             for ff, zz in ((f_cot, z_cot), (f_sg, z_sg))
         ]
     )
-    grad_conv, grad_in, x = lax.psum((local_conv, local_in, x), "rx")
+    flat = jnp.concatenate([local_conv.reshape(-1), local_in.reshape(-1), x.reshape(-1)])
+    unit = devices * 8 * 128
+    flat = jnp.pad(flat, (0, -flat.shape[0] % unit)).reshape(devices, -1, 128)
+    flat = remote_call(
+        sum_kernel, devices, 1, 2, pltpu.VMEM(flat.shape, F32),
+        jax.ShapeDtypeStruct(flat.shape, F32), flat,
+    ).reshape(-1)
+    n_conv, n_in = local_conv.size, local_in.size
+    grad_conv = flat[:n_conv].reshape(local_conv.shape)
+    grad_in = flat[n_conv : n_conv + n_in].reshape(local_in.shape)
+    x = flat[n_conv + n_in : n_conv + n_in + x.size].reshape(x.shape)
     grad_out = read_weights[:, None] * x[0][None] + mix_weights[:, None] * x[1][None]
     return (predicted[:, None], grad_conv, grad_in, grad_out, grad_down, grad_up)
 

time: 453 us -> 260 us (0.57); the launches traced: 444 us -> 256 us
  waiting for transfers between devices: 121 us -> 0.02 us
  Pallas kernels: 0 us -> 67.8 us
  local copies, waits for them, and re-layouts: 107 us -> 41.4 us
  blocking collectives: 56.2 us -> 0 us
  other arithmetic: 37.9 us -> 21.1 us
    psum x1 -> x0, waiting for transfers between devices: 83.3 us -> none  [per_device(): grad_conv, grad_in, x = lax.psum((local_conv, local_in, x), 'rx')]
    pallas_call x0 -> x4, Pallas kernels: none -> 67.8 us  [the longest x2 66.9 us: remote_call(): pl.pallas_call(functools.partial(kernel, devices), out_shape=out_shape, i...]
    reduce_scatter x1 -> x0, waiting for transfers between devices: 38.2 us -> none  [per_device(): lax.psum_scatter(jnp.concatenate([partial.reshape(devices, -1, nt), parti...]
    unnamed x1 -> x0, blocking collectives: 35.2 us -> none
    reshape x6 -> x5, local copies, waits for them, and re-layouts: 36 us -> 1.64 us  [the longest x1 0.72 us: per_device(): grad_conv = flat[:n_conv].reshape(local_conv.shape)]
    all_gather x1 -> x0, blocking collectives: 21.1 us -> none  [per_device(): shared = lax.all_gather(jnp.stack([act, bg]).astype(BF), 'rx')]
    unnamed x140 -> x79, local copies, waits for them, and re-layouts: 22 us -> 8.65 us
    concatenate x6 -> x1, local copies, waits for them, and re-layouts: 12.7 us -> 0.01 us  [per_device(): jnp.concatenate([p_local, q_local, jnp.broadcast_to(tally, (nn, 128))], a...]
  transfers between devices with their start and end apart: 4 -> 1, of which waited for: 2 -> 0; matrix products, arithmetic and copies ran while one was open for 30% -> 31% of each run, Pallas kernels for 0% -> 0%
where the time goes in v2:
time: 260 us; the launch traced here: 256 us
  matrix products  108 us (42%)
  Pallas kernels  67.8 us (26%)
  local copies, waits for them, and re-layouts  41.4 us (16%)
  other arithmetic  21.1 us (8%)
  between operations  17.1 us (7%)
    pallas_call x2, Pallas kernels, remote_call(): pl.pallas_call(functools.partial(kernel, devices), out_shape=out_shape, i...  66.9 us
    dot_general x26, matrix products, high(): return jnp.dot(a, b, precision=HIGH)  26.6 us
    dot_general x18, matrix products, low(): lax.dot_general(a.astype(BF), b.astype(BF), (dims, ((), ())), preferred_e...  23.3 us
    dot_general x2, matrix products, per_device(): jnp.einsum('qcn,n->qc', ip, v, precision=HIGH)  13.1 us
    dot_general x1, matrix products, per_device(): jnp.einsum('rdt,rxt->dx', pre_grad, h1s, preferred_element_type=F32)  11.8 us
    dot_general x1, matrix products, per_device(): jnp.einsum('dx,rxt->rdt', wide_taps, h1s, preferred_element_type=F32)  9.11 us
    unnamed x79, local copies, waits for them, and re-layouts  8.65 us
    dot_general x1, matrix products, per_device(): back = jnp.einsum('qjc,jt->qct', kmat, s, preferred_element_type=F32)  6.71 us
  transfers between devices with their start and end apart: 1, of which 0 were waited for; matrix products, arithmetic and copies ran while one was open for 31% of the time, Pallas kernels for 0%

profile of v2, /device:TPU:0, one launch (start us, length us, event | category | flops | bytes accessed | tf_op | source)
XLA Modules:
  0.0 255.6 jit_solution(1516710965514991046)
XLA Ops:
  7.2 1.3 convert_reduce_fusion.2
  9.2 1.3 multiply_reduce_fusion.1
  19.8 2.0 fusion.201
  21.9 2.5 concatenate.97
  24.4 2.8 %copy.64 = f32[8192,64]{1,0:T(8,128)} copy(f32[8192,64]{0,1:T(8,128)S(1)} %concatenate.97) | data formatting | bytes 4194304 | tf_op jit(solution)/shard_map/concatenate | solution.py:44
  27.3 4.1 %fusion.184 = (f32[64,64,64]{2,1,0:T(8,128)S(1)}, f32[64,64,64]{2,1,0:T(8,128)}) fusion(f32[64,128,64]{2,1,0:T(8,128)} %bitcast.275), kind=kLoop, calls=%fused_computation.263 | loop fusion | bytes 4194304 | tf_op jit(solution)/shard_map/slice | solution.py:189
  31.4 1.3 copy-done.3
  32.7 2.5 fusion.99
  38.6 6.6 %fusion.133 = f32[1,64,64]{2,0,1:T(1,128)S(1)} fusion(f32[1,64]{1,0:T(1,128)S(1)} %fusion.147, f32[64,128,64]{2,1,0:T(8,128)} %bitcast.276), kind=kOutput, calls=%fused_computation.201 | convolution fusion | flops 3145728 | bytes 2113792 | tf_op jit(solution)/shard_map/qcn,n->qc/dot_general | solution.py:202
  45.2 6.6 %fusion.137 = f32[1,64,64]{2,0,1:T(1,128)S(1)} fusion(f32[1,64]{1,0:T(1,128)S(1)} %fusion.149, f32[64,128,64]{2,1,0:T(8,128)} %bitcast.277), kind=kOutput, calls=%fused_computation.205 | convolution fusion | flops 3145728 | bytes 2113792 | tf_op jit(solution)/shard_map/qcn,n->qc/dot_general | solution.py:202
  54.3 3.6 %multiply_convert_fusion = bf16[64,64,512]{2,1,0:T(8,128)(2,1)S(1)} fusion(f32[64,512]{1,0:T(8,128)S(1)} %concatenate.101, f32[64]{0:T(128)S(1)} %get-tuple-element.55, f32[64,512]{1,0:T(8,128)S(1)} %fusion.56, f32[64]{0:T(128)S(1)} %get-tuple-element.56, f32[64,512]{1,0:T(8,128)S(1)} %concatenate.100, f32[64]{0:T(128)S(1)} %get-tuple-element.54, ...), kind=kLoop, calls=%fused_computation.15 | loop fusion | flops 20971520 | bytes 4588544 | tf_op jit(solution)/shard_map/convert_element_type | solution.py:251
  57.9 2.6 %fusion.185 = (bf16[64,64,508]{2,1,0:T(8,128)(2,1)S(1)}, bf16[64,64,508]{2,1,0:T(8,128)(2,1)S(1)}) fusion(bf16[64,64,512]{2,1,0:T(8,128)(2,1)S(1)} %multiply_convert_fusion), kind=kLoop, calls=%fused_computation.264 | loop fusion | bytes 16646144 | tf_op jit(solution)/shard_map/slice | solution.py:26
  60.5 2.0 fusion.20
  62.5 9.1 %convert_reduce_fusion = (f32[64,64]{1,0:T(8,128)S(1)}, bf16[64,64,512]{2,1,0:T(8,128)(2,1)}, f32[64,512,64]{1,2,0:T(8,128)}) fusion(f32[64,512]{1,0:T(8,128)S(1)} %concatenate.101, f32[64]{0:T(128)S(1)} %get-tuple-element.55, f32[64,512]{1,0:T(8,128)S(1)} %fusion.56, f32[64]{0:T(128)S(1)} %get-tuple-element.56, f32[64,512]{1,0:T(8,128)S(1)} %concatenate.100, ...), kind=kOutput, calls=%fused_computation.12 | convolution fusion | flops 905965568 | bytes 25535488 | tf_op jit(solution)/shard_map/dx,rxt->rdt/dot_general | solution.py:254
  71.7 1.1 pad_maximum_fusion.2
  74.3 1.8 rev.16
  76.1 1.8 copy.73
  77.9 1.8 stack_reshape.9
  79.7 2.3 rev.10
  82.5 1.8 fusion.186
  84.3 2.3 copy.95
  86.6 2.7 %copy.96 = bf16[64,64,64]{1,2,0:T(8,128)(2,1)} copy(bf16[64,64,64]{2,1,0:T(8,128)(2,1)} %get-tuple-element.45) | data formatting | bytes 1048576
  89.3 1.8 fusion.39
  91.1 5.0 %fusion.191 = (f32[192]{0:T(256)S(1)}, f32[192,512]{1,0:T(8,128)S(1)}) fusion(bf16[64,64,512]{2,1,0:T(8,128)(2,1)} %get-tuple-element.37, bf16[64,64,64]{1,2,0:T(8,128)(2,1)S(1)} %fusion.39, bf16[64,64,64]{1,2,0:T(8,128)(2,1)} %copy.96, bf16[64,64,64]{1,2,0:T(8,128)(2,1)} %copy.95), kind=kOutput, calls=%fused_computation.270 | convolution fusion | flops 810123072 | bytes 6161152 | tf_op jit(solution)/shard_map/dot_general | solution.py:34
  98.3 7.2 %fusion.131 = f32[1,64,64]{2,0,1:T(1,128)} fusion(f32[1,64]{1,0:T(1,128)S(1)} %fusion.147, f32[64,128,64]{2,1,0:T(8,128)} %bitcast.278), kind=kOutput, calls=%fused_computation.199 | convolution fusion | flops 3145728 | bytes 2113792 | tf_op jit(solution)/shard_map/dot_general | solution.py:30
  105.5 7.2 %fusion.135 = f32[1,64,64]{2,0,1:T(1,128)} fusion(f32[1,64]{1,0:T(1,128)S(1)} %fusion.149, f32[64,128,64]{2,1,0:T(8,128)} %bitcast.279), kind=kOutput, calls=%fused_computation.203 | convolution fusion | flops 3145728 | bytes 2113792 | tf_op jit(solution)/shard_map/dot_general | solution.py:30
  112.7 2.8 %fusion.139 = f32[1,64,512]{2,0,1:T(1,128)S(1)} fusion(bf16[64,64,512]{2,1,0:T(8,128)(2,1)} %get-tuple-element.37, f32[64]{0:T(128)S(1)} %copy-done.33), kind=kOutput, calls=%fused_computation.207 | convolution fusion | flops 4194368 | bytes 4325632 | tf_op jit(solution)/shard_map/c,rct->rt/dot_general | solution.py:256
  115.6 2.4 fusion.145
  119.7 1.3 compare_select_fusion.4
  121.0 2.1 fusion.21
  123.8 1.2 fusion.124
  124.9 1.9 fusion.19
  126.8 1.8 copy.72
  128.6 1.8 stack_reshape.8
  131.5 49.1 %shard_map.200 = (bf16[16,2,64,128]{3,2,1,0:T(8,128)(2,1)S(1)}, bf16[16,64,512]{2,1,0:T(8,128)(2,1)S(1)}) custom-call(bf16[16,2,64,128]{3,2,1,0:T(8,128)(2,1)S(1)} %pad_maximum_fusion.3.x_ref, bf16[64,512]{1,0:T(8,128)(2,1)S(1)} %slice.210.y_ref), custom_call_target="tpu_custom_call" | custom-call | tf_op jit(solution)/shard_map/pallas_call | solution.py:157
  180.6 1.5 fusion.28
  183.7 1.1 reshape_squeeze.7
  184.8 1.9 fusion.31
  190.7 6.7 %fusion.193 = (f32[64,64]{1,0:T(8,128)S(1)}, f32[64,64,512]{2,1,0:T(8,128)}) fusion(bf16[64,512]{1,0:T(8,128)(2,1)S(1)} %fusion.27, bf16[64,512]{1,0:T(8,128)(2,1)} %bitcast.284, bf16[64,512]{1,0:T(8,128)(2,1)S(1)} %get-tuple-element.64, bf16[64,64,64]{1,2,0:T(8,128)(2,1)} %copy-done.5, bf16[64,64,64]{1,2,0:T(8,128)(2,1)} %copy.96, ...), kind=kOutput, calls=%fused_computation.272 | convolution fusion | flops 812707840 | bytes 10174464 | tf_op jit(solution)/shard_map/qjc,jt->qct/dot_general | solution.py:290
  197.5 3.7 %bitcast_subtract_fusion = f32[64,192,64]{2,1,0:T(8,128)S(1)} fusion(f32[64,64]{1,0:T(8,128)S(1)} %copy-done.31, f32[192]{0:T(256)S(1)} %convert_reduce_fusion.1, bf16[64,64,512]{2,1,0:T(8,128)(2,1)} %get-tuple-element.37, bf16[64,512]{1,0:T(8,128)(2,1)} %copy-done.17, bf16[64,512]{1,0:T(8,128)(2,1)S(1)} %bitcast.285, bf16[64,512]{1,0:T(8,128)(2,1)} %copy-done.15), kind=kOutput, calls=%fused_computation.16 | convolution fusion | flops 807469056 | bytes 7553792 | tf_op jit(solution)/shard_map/jt,qct->qjc/dot_general | solution.py:299
  203.9 2.8 %convolution_bitcast_fusion.7 = f32[64]{0:T(128)S(1)} fusion(f32[64,64,1]{1,2,0:T(1,128)S(1)} %bitcast.296, f32[64,128,64]{2,1,0:T(8,128)} %bitcast.280), kind=kOutput, calls=%fused_computation.68 | convolution fusion | flops 3145728 | bytes 2113792 | tf_op jit(solution)/shard_map/qcn,qc->n/dot_general | solution.py:319
  206.8 2.8 %convolution_bitcast_fusion.5 = f32[64]{0:T(128)S(1)} fusion(f32[64,64,1]{1,2,0:T(1,128)S(1)} %bitcast.295, f32[64,128,64]{2,1,0:T(8,128)} %bitcast.281), kind=kOutput, calls=%fused_computation.64 | convolution fusion | flops 3145728 | bytes 2113792 | tf_op jit(solution)/shard_map/qcn,qc->n/dot_general | solution.py:319
  209.6 1.2 fusion.38
  210.8 1.2 fusion.36
  212.3 11.8 %fusion.8 = f32[64,192,1]{0,1,2:T(8,128)S(1)} fusion(f32[64,512,64]{1,2,0:T(8,128)} %get-tuple-element.61, f32[64,64,512]{2,1,0:T(8,128)} %get-tuple-element.67, f32[64,64]{1,0:T(8,128)S(1)} %broadcast_multiply_fusion.1, f32[64,512]{1,0:T(8,128)S(1)} %copy-done.26, f32[64]{0:T(128)S(1)} %copy-done.33, f32[64,512]{1,0:T(8,128)S(1)} %copy-done.25, ...), kind=kOutput, calls=%fused_computation.17 | convolution fusion | flops 897581056 | bytes 29622784 | tf_op jit(solution)/shard_map/rdt,rxt->dx/dot_general | solution.py:297
  224.3 17.8 %shard_map.202 = f32[16,16,128]{2,1,0:T(8,128)S(1)} custom-call(f32[16,16,128]{2,1,0:T(8,128)S(1)} %bitcast.273), custom_call_target="tpu_custom_call" | custom-call | tf_op jit(solution)/shard_map/pallas_call | solution.py:157
  242.3 1.4 fusion.74
  243.7 1.1 convolution_add_fusion.2
  (175 shorter events, 33.8 us)
Async XLA Ops:
  7.2 29.5 %copy-start = (bf16[256,64]{0,1:T(8,128)(2,1)S(1)}, bf16[256,64]{0,1:T(8,128)(2,1)}, u32[]{:S(2)}) copy-start(bf16[256,64]{0,1:T(8,128)(2,1)} %param.30) | copy-start | bytes 98308
  7.2 110.8 %all-gather.2.cloned.1.call-start = ((), (), s32[]{:S(2)}) async-start(), calls=%async_computation | async-start | bytes 1949696 | tf_op jit(solution)/shard_map/all_gather | solution.py:220
  27.2 9.7 %copy-start.8 = (bf16[64,1,512]{2,0,1:T(8,128)(2,1)S(1)}, bf16[64,1,512]{2,0,1:T(8,128)(2,1)}, u32[]{:S(2)}) copy-start(bf16[64,1,512]{2,0,1:T(8,128)(2,1)} %param.17) | copy-start | bytes 196612
  27.2 11.2 %copy-start.36 = (s32[64]{0:T(128)S(1)}, s32[64]{0:T(128)}, u32[]{:S(2)}) copy-start(s32[64]{0:T(128)} %param.19) | copy-start | bytes 772
  27.2 11.2 %copy-start.20 = (bf16[64,1,512]{2,0,1:T(8,128)(2,1)S(1)}, bf16[64,1,512]{2,0,1:T(8,128)(2,1)}, u32[]{:S(2)}) copy-start(bf16[64,1,512]{2,0,1:T(8,128)(2,1)} %param.16) | copy-start | bytes 196612
  31.4 1.3 copy-start.3
  31.4 20.3 %copy-start.32 = (f32[64]{0:T(128)S(1)}, f32[64]{0:T(128)}, u32[]{:S(2)}) copy-start(f32[64]{0:T(128)} %param.29) | copy-start | bytes 772
  31.4 20.4 %copy-start.37 = (f32[64]{0:T(128)S(1)}, f32[64]{0:T(128)}, u32[]{:S(2)}) copy-start(f32[64]{0:T(128)} %param.28) | copy-start | bytes 772
  31.4 21.0 %copy-start.34 = (f32[3,64]{1,0:T(4,128)S(1)}, f32[3,64]{1,0:T(4,128)}, u32[]{:S(2)}) copy-start(f32[3,64]{1,0:T(4,128)} %param.20) | copy-start | bytes 2308
  31.4 21.9 %copy-start.30 = (bf16[3,64,64]{2,1,0:T(8,128)(2,1)S(1)}, bf16[3,64,64]{2,1,0:T(8,128)(2,1)}, u32[]{:S(2)}) copy-start(bf16[3,64,64]{2,1,0:T(8,128)(2,1)} %param.22) | copy-start | bytes 73732
  35.2 19.1 %copy-start.35 = (f32[64]{0:T(128)S(1)}, f32[64]{0:T(128)}, u32[]{:S(2)}) copy-start(f32[64]{0:T(128)} %param.21) | copy-start | bytes 772
  36.7 1.1 copy-start.19
  54.3 17.4 %copy-start.11 = (f32[1024,64]{1,0:T(8,128)}, f32[1024,64]{1,0:T(8,128)S(1)}, u32[]{:S(2)}) copy-start(f32[1024,64]{1,0:T(8,128)S(1)} %copy.94) | copy-start | bytes 786436
  57.8 4.7 %copy-start.2 = (bf16[64,64,512]{2,1,0:T(8,128)(2,1)}, bf16[64,64,512]{2,1,0:T(8,128)(2,1)S(1)}, u32[]{:S(2)}) copy-start(bf16[64,64,512]{2,1,0:T(8,128)(2,1)S(1)} %multiply_convert_fusion) | copy-start | bytes 12582916
  57.9 2.6 %copy-start.27 = (bf16[64,256]{1,0:T(8,128)(2,1)S(1)}, bf16[64,256]{1,0:T(8,128)(2,1)}, u32[]{:S(2)}) copy-start(bf16[64,256]{1,0:T(8,128)(2,1)} %param.31) | copy-start | bytes 98308
  60.5 11.2 %copy-start.6 = (bf16[64,64,508]{2,1,0:T(8,128)(2,1)}, bf16[64,64,508]{2,1,0:T(8,128)(2,1)S(1)}, u32[]{:S(2)}) copy-start(bf16[64,64,508]{2,1,0:T(8,128)(2,1)S(1)} %get-tuple-element.42) | copy-start | bytes 12484612
  60.5 11.2 %copy-start.7 = (bf16[64,64,508]{2,1,0:T(8,128)(2,1)}, bf16[64,64,508]{2,1,0:T(8,128)(2,1)S(1)}, u32[]{:S(2)}) copy-start(bf16[64,64,508]{2,1,0:T(8,128)(2,1)S(1)} %get-tuple-element.43) | copy-start | bytes 12484612
  91.1 5.0 %copy-start.5 = (bf16[64,64,64]{1,2,0:T(8,128)(2,1)}, bf16[64,64,64]{1,2,0:T(8,128)(2,1)S(1)}, u32[]{:S(2)}) copy-start(bf16[64,64,64]{1,2,0:T(8,128)(2,1)S(1)} %fusion.39) | copy-start | bytes 1572868
  91.1 21.6 %copy-start.33 = (f32[64]{0:T(128)S(1)}, f32[64]{0:T(128)}, u32[]{:S(2)}) copy-start(f32[64]{0:T(128)} %param.27) | copy-start | bytes 772
  96.3 0.7 copy-start.10
  97.0 18.5 %copy-start.4 = (bf16[64,64,512]{2,1,0:T(8,128)(2,1)S(1)}, bf16[64,64,512]{2,1,0:T(8,128)(2,1)}, u32[]{:S(2)}) copy-start(bf16[64,64,512]{2,1,0:T(8,128)(2,1)} %get-tuple-element.37) | copy-start | bytes 12582916
  115.6 66.5 %copy-start.14 = (f32[1,64,512]{2,0,1:T(1,128)}, f32[1,64,512]{2,0,1:T(1,128)S(1)}, u32[]{:S(2)}) copy-start(f32[1,64,512]{2,0,1:T(1,128)S(1)} %fusion.139) | copy-start | bytes 393220
  123.1 0.7 copy-start.29
  182.1 4.7 %copy-start.12 = (bf16[64,512]{1,0:T(8,128)(2,1)}, bf16[64,512]{1,0:T(8,128)(2,1)S(1)}, u32[]{:S(2)}) copy-start(bf16[64,512]{1,0:T(8,128)(2,1)S(1)} %fusion.28) | copy-start | bytes 196612
  187.9 2.8 %copy-start.17 = (bf16[64,512]{1,0:T(8,128)(2,1)}, bf16[64,512]{1,0:T(8,128)(2,1)S(1)}, u32[]{:S(2)}) copy-start(bf16[64,512]{1,0:T(8,128)(2,1)S(1)} %fusion.27) | copy-start | bytes 196612
  187.9 9.6 %copy-start.9 = (bf16[64,1,512]{2,0,1:T(8,128)(2,1)S(1)}, bf16[64,1,512]{2,0,1:T(8,128)(2,1)}, u32[]{:S(2)}) copy-start(bf16[64,1,512]{2,0,1:T(8,128)(2,1)} %param.17) | copy-start | bytes 196612
  188.7 2.0 copy-start.15
  188.7 8.8 %copy-start.31 = (f32[64,64]{1,0:T(8,128)S(1)}, f32[64,64]{1,0:T(8,128)}, u32[]{:S(2)}) copy-start(f32[64,64]{1,0:T(8,128)} %broadcast_multiply_fusion) | copy-start | bytes 49156
  201.7 1.7 copy-start.21
  201.8 1.9 copy-start.22
  202.2 7.4 %copy-start.23 = (f32[64,64]{1,0:T(8,128)S(1)}, f32[64,64]{1,0:T(8,128)}, u32[]{:S(2)}) copy-start(f32[64,64]{1,0:T(8,128)} %convolution_multiply_fusion.2) | copy-start | bytes 49156
  202.8 9.3 %copy-start.25 = (f32[64,512]{1,0:T(8,128)S(1)}, f32[64,512]{1,0:T(8,128)}, u32[]{:S(2)}) copy-start(f32[64,512]{1,0:T(8,128)} %convert_bitcast_fusion.1) | copy-start | bytes 393220
  202.9 9.3 %copy-start.26 = (f32[64,512]{1,0:T(8,128)S(1)}, f32[64,512]{1,0:T(8,128)}, u32[]{:S(2)}) copy-start(f32[64,512]{1,0:T(8,128)} %get-tuple-element.65) | copy-start | bytes 393220
  212.2 29.9 %copy-start.16 = (bf16[16,1,64,128]{3,2,1,0:T(8,128)(2,1)S(1)}, bf16[16,1,64,128]{3,2,1,0:T(8,128)(2,1)}, u32[]{:S(2)}) copy-start(bf16[16,1,64,128]{3,2,1,0:T(8,128)(2,1)} %get-tuple-element.47) | copy-start | bytes 786436
  212.2 31.5 %copy-start.13 = (bf16[64,512]{1,0:T(8,128)(2,1)S(1)}, bf16[64,512]{1,0:T(8,128)(2,1)}, u32[]{:S(2)}) copy-start(bf16[64,512]{1,0:T(8,128)(2,1)} %copy-done.12) | copy-start | bytes 196612
  212.2 31.5 %copy-start.18 = (f32[1,64,512]{2,0,1:T(1,128)S(1)}, f32[1,64,512]{2,0,1:T(1,128)}, u32[]{:S(2)}) copy-start(f32[1,64,512]{2,0,1:T(1,128)} %fusion.145) | copy-start | bytes 393220
  212.2 31.5 %copy-start.24 = (f32[64,64]{1,0:T(8,128)S(1)}, f32[64,64]{1,0:T(8,128)}, u32[]{:S(2)}) copy-start(f32[64,64]{1,0:T(8,128)} %reshape.250) | copy-start | bytes 49156
  212.2 32.6 %copy-start.28 = (bf16[64,256]{1,0:T(8,128)(2,1)S(1)}, bf16[64,256]{1,0:T(8,128)(2,1)}, u32[]{:S(2)}) copy-start(bf16[64,256]{1,0:T(8,128)(2,1)} %param.31) | copy-start | bytes 98308
  212.2 36.3 %copy-start.1 = (bf16[256,64]{0,1:T(8,128)(2,1)S(1)}, bf16[256,64]{0,1:T(8,128)(2,1)}, u32[]{:S(2)}) copy-start(bf16[256,64]{0,1:T(8,128)(2,1)} %param.30) | copy-start | bytes 98308
Sparse Core Ops, SparseCore 0:
  38.0 43.1 all-gather.1
